TPU v7x, 256 devices: a whole 4x4x8 slice. The times are simulated.
256 devices in a mesh: gx: 8 (over z), gy: 8 (over y_hi, x), col: 4 (over y_lo, core).
Axes of the slice: x: 4, y: 4 (y_hi: 2, y_lo: 2; y = y_hi * 2 + y_lo), z: 8, core: 2. Of those that a mesh axis runs over, the one named last changes fastest.
Arguments:
- volume: bfloat16 [1, 128, 64, 64, 128], P(None, 'col', 'gx', 'gy'), may hold values from -6 to 6
- weight_one: bfloat16 [3, 3, 3, 128, 128], P(None, None, None, 'col'), may hold values from -0.109375 to 0.109375
- bias_one: float32 [128], P('col'), may hold values from -3 to 3
- weight_two: bfloat16 [3, 3, 3, 128, 128], P(None, None, None, 'col'), may hold values from -0.109375 to 0.109375
- bias_two: float32 [128], P('col'), may hold values from -3 to 3
Outputs:
- activations: bfloat16 [1, 128, 64, 64, 128], P(None, 'col', 'gx', 'gy')
All inputs are finite; a program needn't handle non-finite values.
Results may differ from a plain program's by a relative error of at most 0.01.
Values may be sent and summed in bfloat16 or wider, within the bound.
A program may use at most 64 MiB of HBM per device.

v0:
```python
import jax
import jax.numpy as jnp
from jax import lax
from jax.sharding import PartitionSpec as P


def with_halo(cells, sides, width):
    for axis, dim in sides:
        count = lax.axis_size(axis)
        head = lax.slice_in_dim(cells, 0, width, axis=dim)
        tail = lax.slice_in_dim(cells, cells.shape[dim] - width, cells.shape[dim], axis=dim)
        cells = jnp.concatenate(
            [
                lax.ppermute(tail, axis, [(i, (i + 1) % count) for i in range(count)]),
                cells,
                lax.ppermute(head, axis, [((i + 1) % count, i) for i in range(count)]),
            ],
            axis=dim,
        )
    return cells


def depth_terms(padded, weight):
    cells_x = padded.shape[2] - 2
    cells_y = padded.shape[3] - 2
    running = jnp.zeros(
        (padded.shape[0], 3, weight.shape[3], cells_x, cells_y, padded.shape[4]), jnp.float32
    )
    for step_x in range(3):
        for step_y in range(3):
            slab = padded[:, :, step_x : step_x + cells_x, step_y : step_y + cells_y, :]
            running = running + jnp.einsum(
                "bixyz,doi->bdoxyz",
                slab,
                weight[step_x, step_y],
                preferred_element_type=jnp.float32,
            )
    return running


def local_conv(padded, weight):
    terms = depth_terms(padded, weight)
    return terms[:, 1] + jnp.roll(terms[:, 0], 1, axis=4) + jnp.roll(terms[:, 2], -1, axis=4)


def finish(total, layer_bias):
    return jax.nn.relu(total + layer_bias[None, :, None, None, None]).astype(jnp.bfloat16)


def conv_layer(volume, weight, layer_bias):
    gathered = lax.all_gather(volume, "col", axis=1, tiled=True)
    padded = with_halo(gathered, (("gx", 2), ("gy", 3)), 1)
    total = local_conv(padded, weight)
    return finish(total, layer_bias)


def local(volume, weight_one, bias_one, weight_two, bias_two):
    hidden = conv_layer(volume, weight_one, bias_one)
    return conv_layer(hidden, weight_two, bias_two)


def solution(mesh):
    in_specs = (
        P(None, "col", "gx", "gy", None),
        P(None, None, None, "col", None),
        P("col"),
        P(None, None, None, "col", None),
        P("col"),
    )
    out_specs = P(None, "col", "gx", "gy", None)
    return jax.shard_map(local, mesh=mesh, in_specs=in_specs, out_specs=out_specs, check_vma=False)
```

profile of v0, /device:TPU:1, one launch (start us, length us, event | category | flops | bytes accessed | tf_op | source)
XLA Modules:
  0.0 165.8 jit_solution(17004797147646809525)
XLA Ops:
  6.5 2.2 %copy.6 = bf16[1,32,8,8,128]{4,1,3,2,0:T(8,128)(2,1)} copy(bf16[1,32,8,8,128]{4,3,2,1,0:T(8,128)(2,1)} %param.5) | data formatting | bytes 1048576 | tf_op args[0]
  8.8 36.3 %all-gather.3.cloned.1.call-done = bf16[1,128,8,8,128]{4,1,3,2,0:T(8,128)(2,1)} async-done(((bf16[1,32,8,8,128]{4,1,3,2,0:T(8,128)(2,1)}), bf16[1,128,8,8,128]{4,1,3,2,0:T(8,128)(2,1)}) %all-gather.3.cloned.1.call-update) | async-done | bytes 2097168 | tf_op jit(solution)/shard_map/all_gather | solution.py:51
  45.1 1.1 fusion.138
  46.2 1.4 collective-permute-start
  47.5 1.8 %collective-permute-start.1 = (bf16[1,128,1,8,128]{4,1,3,2,0:T(8,128)(2,1)S(1)}, bf16[1,128,1,8,128]{4,1,3,2,0:T(8,128)(2,1)S(1)}, u32[]{:S(2)}, u32[]{:S(2)}) collective-permute-start(bf16[1,128,1,8,128]{4,1,3,2,0:T(8,128)(2,1)S(1)} %get-tuple-element.16), channel_id=1, source_target_pairs={{32,0},{64,32},{96,64},{128,96},{160,128},{192,160},{224,192},{0,2... | collective-permute-start | bytes 786440 | tf_op jit(solution)/shard_map/ppermute | solution.py:16
  49.4 2.2 %fusion.65 = f32[3,32,8,8,128]{4,1,0,3,2:T(8,128)S(1)} fusion(bf16[1,128,8,8,128]{4,1,3,2,0:T(8,128)(2,1)} %all-gather.3.cloned.1.call-done, bf16[3,3,3,32,128]{4,3,2,1,0:T(8,128)(2,1)} %param.6), kind=kOutput, calls=%fused_computation.79 | convolution fusion | flops 201326592 | bytes 5267456 | tf_op jit(solution)/shard_map/bixyz,doi->bdoxyz/dot_general | solution.py:32
  51.6 4.3 %collective-permute-done = bf16[1,128,1,8,128]{4,1,3,2,0:T(8,128)(2,1)S(1)} collective-permute-done((bf16[1,128,1,8,128]{4,1,3,2,0:T(8,128)(2,1)S(1)}, bf16[1,128,1,8,128]{4,1,3,2,0:T(8,128)(2,1)S(1)}, u32[]{:S(2)}, u32[]{:S(2)}) %collective-permute-start) | collective-permute-done | bytes 262176 | tf_op jit(solution)/shard_map/ppermute | solution.py:14
  56.3 4.6 %collective-permute-start.3 = (bf16[1,128,10,1,128]{4,1,3,2,0:T(8,128)(2,1)S(1)}, bf16[1,128,10,1,128]{4,1,3,2,0:T(8,128)(2,1)S(1)}, u32[]{:S(2)}, u32[]{:S(2)}) collective-permute-start(bf16[1,128,10,1,128]{4,1,3,2,0:T(8,128)(2,1)S(1)} %get-tuple-element.11), channel_id=1, source_target_pairs={{4,0},{8,4},{12,8},{16,12},{20,16},{24,20},{28,24},{0,28},{5,1},{9... | collective-permute-start | bytes 983048 | tf_op jit(solution)/shard_map/ppermute | solution.py:16
  61.0 2.2 %fusion.54 = f32[8,8,128,3,32]{2,4,3,1,0:T(8,128)} fusion(bf16[1,128,1,8,128]{4,1,3,2,0:T(8,128)(2,1)S(1)} %collective-permute-done.1, bf16[1,128,8,8,128]{4,1,3,2,0:T(8,128)(2,1)S(1)} %copy-done, bf16[3,3,3,32,128]{4,3,2,1,0:T(8,128)(2,1)S(1)} %copy-done.2), kind=kOutput, calls=%fused_computation.69 | convolution fusion | flops 205520896 | bytes 5529600 | tf_op jit(solution)/shard_map/bixyz,doi->bdoxyz/dot_general | solution.py:32
  63.2 2.2 %fusion.62 = f32[8,8,128,3,32]{2,4,3,1,0:T(8,128)} fusion(bf16[1,128,8,8,128]{4,1,3,2,0:T(8,128)(2,1)S(1)} %copy-done, bf16[1,128,1,8,128]{4,1,3,2,0:T(8,128)(2,1)S(1)} %collective-permute-done, bf16[3,3,3,32,128]{4,3,2,1,0:T(8,128)(2,1)S(1)} %copy-done.2), kind=kOutput, calls=%fused_computation.77 | convolution fusion | flops 205520896 | bytes 5529600 | tf_op jit(solution)/shard_map/bixyz,doi->bdoxyz/dot_general | solution.py:32
  65.4 7.5 %collective-permute-done.2 = bf16[1,128,10,1,128]{4,1,3,2,0:T(8,128)(2,1)S(1)} collective-permute-done((bf16[1,128,10,1,128]{4,1,3,2,0:T(8,128)(2,1)S(1)}, bf16[1,128,10,1,128]{4,1,3,2,0:T(8,128)(2,1)S(1)}, u32[]{:S(2)}, u32[]{:S(2)}) %collective-permute-start.2) | collective-permute-done | bytes 327712 | tf_op jit(solution)/shard_map/ppermute | solution.py:14
  72.9 0.6 fusion.31
  73.4 0.6 fusion.58
  74.0 0.6 fusion.27
  75.7 5.4 %fusion = f32[1,3,32,8,8,128]{5,2,1,4,3,0:T(8,128)} fusion(f32[8,8,128,3,32]{2,4,3,1,0:T(8,128)} %fusion.54, f32[8,8,128,3,32]{2,4,3,1,0:T(8,128)S(1)} %fusion.58, f32[8,8,128,3,32]{2,4,3,1,0:T(8,128)S(1)} %fusion.19, f32[3,32,8,8,128]{4,1,0,3,2:T(8,128)S(1)} %fusion.65, f32[8,8,128,3,32]{2,4,3,1,0:T(8,128)S(1)} %fusion.27, ...), kind=kOutput, calls=%fused_computation.9 | convolution fusion | flops 211812352 | bytes 31285248 | tf_op jit(solution)/shard_map/bixyz,doi->bdoxyz/dot_general | solution.py:32
  81.1 1.7 %slice_bitcast_fusion.3 = (f32[1,32,8,8,128]{4,1,3,2,0:T(8,128)S(1)}, f32[1,32,8,8,128]{4,1,3,2,0:T(8,128)S(1)}) fusion(f32[1,3,32,8,8,128]{5,2,1,4,3,0:T(8,128)} %fusion), kind=kLoop, calls=%fused_computation.91 | loop fusion | bytes 4194304 | tf_op jit(solution)/shard_map/squeeze | solution.py:43
  83.5 2.7 %fusion.82 = bf16[1,32,8,8,128]{4,1,3,2,0:T(8,128)(2,1)} fusion(f32[1,3,32,8,8,128]{5,2,1,4,3,0:T(8,128)} %fusion, f32[1,32,8,8,127]{4,1,3,2,0:T(8,128)S(1)} %bitcast.287, f32[1,32,8,8,1]{4,1,3,2,0:T(8,128)S(1)} %slice.258, f32[1,32,8,8,1]{4,1,3,2,0:T(8,128)S(1)} %bitcast.286, f32[1,32,8,8,127]{4,1,3,2,0:T(8,128)S(1)} %slice.261, f32[32]{0:T(128)S(1)} %copy-done.4), kind=kLoop, calls=%fused_computation.98 | loop fusion | flops 1835008 | bytes 3670144 | tf_op jit(solution)/shard_map/convert_element_type | solution.py:47
  86.3 29.5 %all-gather.5.cloned.1.call-done = bf16[1,128,8,8,128]{4,1,3,2,0:T(8,128)(2,1)} async-done(((bf16[1,32,8,8,128]{4,1,3,2,0:T(8,128)(2,1)}), bf16[1,128,8,8,128]{4,1,3,2,0:T(8,128)(2,1)}) %all-gather.5.cloned.1.call-update) | async-done | bytes 2097168 | tf_op jit(solution)/shard_map/all_gather | solution.py:51
  115.8 1.1 fusion.137
  116.9 1.4 collective-permute-start.4
  118.3 2.0 %collective-permute-start.5 = (bf16[1,128,1,8,128]{4,1,3,2,0:T(8,128)(2,1)S(1)}, bf16[1,128,1,8,128]{4,1,3,2,0:T(8,128)(2,1)S(1)}, u32[]{:S(2)}, u32[]{:S(2)}) collective-permute-start(bf16[1,128,1,8,128]{4,1,3,2,0:T(8,128)(2,1)S(1)} %get-tuple-element.14), channel_id=1, source_target_pairs={{32,0},{64,32},{96,64},{128,96},{160,128},{192,160},{224,192},{0,2... | collective-permute-start | bytes 786440 | tf_op jit(solution)/shard_map/ppermute | solution.py:16
  120.3 2.1 %fusion.67 = f32[8,8,128,3,32]{2,4,1,0,3:T(8,128)S(1)} fusion(bf16[1,128,8,8,128]{4,1,3,2,0:T(8,128)(2,1)} %all-gather.5.cloned.1.call-done, bf16[3,3,3,32,128]{4,3,2,1,0:T(8,128)(2,1)S(1)} %copy-done.3), kind=kOutput, calls=%fused_computation.81 | convolution fusion | flops 201326592 | bytes 5267456 | tf_op jit(solution)/shard_map/bixyz,doi->bdoxyz/dot_general | solution.py:32
  122.5 4.2 %collective-permute-done.4 = bf16[1,128,1,8,128]{4,1,3,2,0:T(8,128)(2,1)S(1)} collective-permute-done((bf16[1,128,1,8,128]{4,1,3,2,0:T(8,128)(2,1)S(1)}, bf16[1,128,1,8,128]{4,1,3,2,0:T(8,128)(2,1)S(1)}, u32[]{:S(2)}, u32[]{:S(2)}) %collective-permute-start.4) | collective-permute-done | bytes 262176 | tf_op jit(solution)/shard_map/ppermute | solution.py:14
  127.0 4.6 %collective-permute-start.7 = (bf16[1,128,10,1,128]{4,1,3,2,0:T(8,128)(2,1)S(1)}, bf16[1,128,10,1,128]{4,1,3,2,0:T(8,128)(2,1)S(1)}, u32[]{:S(2)}, u32[]{:S(2)}) collective-permute-start(bf16[1,128,10,1,128]{4,1,3,2,0:T(8,128)(2,1)S(1)} %get-tuple-element.9), channel_id=1, source_target_pairs={{4,0},{8,4},{12,8},{16,12},{20,16},{24,20},{28,24},{0,28},{5,1},{9... | collective-permute-start | bytes 983048 | tf_op jit(solution)/shard_map/ppermute | solution.py:16
  131.7 0.6 fusion.38
  132.8 10.8 %collective-permute-done.6 = bf16[1,128,10,1,128]{4,1,3,2,0:T(8,128)(2,1)S(1)} collective-permute-done((bf16[1,128,10,1,128]{4,1,3,2,0:T(8,128)(2,1)S(1)}, bf16[1,128,10,1,128]{4,1,3,2,0:T(8,128)(2,1)S(1)}, u32[]{:S(2)}, u32[]{:S(2)}) %collective-permute-start.6) | collective-permute-done | bytes 327712 | tf_op jit(solution)/shard_map/ppermute | solution.py:14
  144.7 2.2 %fusion.11 = f32[8,8,128,3,32]{2,4,1,0,3:T(8,128)} fusion(bf16[1,128,10,8,128]{4,1,3,2,0:T(8,128)(2,1)S(1)} %constant_dynamic-update-slice_fusion.3, bf16[1,128,10,1,128]{4,1,3,2,0:T(8,128)(2,1)S(1)} %collective-permute-done.6, bf16[3,3,3,32,128]{4,3,2,1,0:T(8,128)(2,1)S(1)} %copy-done.3), kind=kOutput, calls=%fused_computation.31 | convolution fusion | flops 205520896 | bytes 6119424 | tf_op jit(solution)/shard_map/bixyz,doi->bdoxyz/dot_general | solution.py:32
  147.0 2.3 %fusion.7 = f32[8,8,128,3,32]{2,4,1,0,3:T(8,128)} fusion(bf16[1,128,10,8,128]{4,1,3,2,0:T(8,128)(2,1)S(1)} %constant_dynamic-update-slice_fusion.3, bf16[1,128,10,1,128]{4,1,3,2,0:T(8,128)(2,1)S(1)} %collective-permute-done.7, bf16[3,3,3,32,128]{4,3,2,1,0:T(8,128)(2,1)S(1)} %copy-done.3), kind=kOutput, calls=%fused_computation.28 | convolution fusion | flops 205520896 | bytes 6119424 | tf_op jit(solution)/shard_map/bixyz,doi->bdoxyz/dot_general | solution.py:32
  149.3 2.2 %fusion.3 = f32[8,8,128,3,32]{2,4,1,0,3:T(8,128)} fusion(bf16[1,128,10,8,128]{4,1,3,2,0:T(8,128)(2,1)S(1)} %constant_dynamic-update-slice_fusion.3, bf16[1,128,10,1,128]{4,1,3,2,0:T(8,128)(2,1)S(1)} %collective-permute-done.7, bf16[3,3,3,32,128]{4,3,2,1,0:T(8,128)(2,1)S(1)} %copy-done.3), kind=kOutput, calls=%fused_computation.25 | convolution fusion | flops 205520896 | bytes 6119424 | tf_op jit(solution)/shard_map/bixyz,doi->bdoxyz/dot_general | solution.py:32
  151.5 4.9 %add_bitcast_fusion = f32[1,3,32,8,8,128]{5,2,4,3,1,0:T(8,128)S(1)} fusion(f32[8,8,128,3,32]{2,4,1,0,3:T(8,128)S(1)} %fusion.38, f32[8,8,128,3,32]{2,4,1,0,3:T(8,128)S(1)} %fusion.42, f32[8,8,128,3,32]{2,4,1,0,3:T(8,128)} %fusion.3, f32[8,8,128,3,32]{2,4,1,0,3:T(8,128)S(1)} %fusion.67, f32[8,8,128,3,32]{2,4,1,0,3:T(8,128)} %fusion.11, ...), kind=kOutput, calls=%fused_computation.14 | convolution fusion | flops 211812352 | bytes 31285248 | tf_op jit(solution)/shard_map/bixyz,doi->bdoxyz/dot_general | solution.py:32
  157.3 0.7 fusion.77
  157.9 1.0 copy.19
  (40 shorter events, 5.3 us)
Async XLA Ops:
  6.5 38.6 %all-gather.3.cloned.1.call-start = ((), (), s32[]{:S(2)}) async-start(), calls=%async_computation | async-start | bytes 2621440 | tf_op jit(solution)/shard_map/all_gather | solution.py:51
  8.7 107.1 %all-gather.5.cloned.1.call-start = ((), (), s32[]{:S(2)}) async-start(), calls=%async_computation.1 | async-start | bytes 2621440 | tf_op jit(solution)/shard_map/all_gather | solution.py:51
  46.2 9.8 %copy-start = (bf16[1,128,8,8,128]{4,1,3,2,0:T(8,128)(2,1)S(1)}, bf16[1,128,8,8,128]{4,1,3,2,0:T(8,128)(2,1)}, u32[]{:S(2)}) copy-start(bf16[1,128,8,8,128]{4,1,3,2,0:T(8,128)(2,1)} %all-gather.3.cloned.1.call-done) | copy-start | bytes 6291460
  46.2 9.7 %collective-permute-start = (bf16[1,128,1,8,128]{4,1,3,2,0:T(8,128)(2,1)S(1)}, bf16[1,128,1,8,128]{4,1,3,2,0:T(8,128)(2,1)S(1)}, u32[]{:S(2)}, u32[]{:S(2)}) collective-permute-start(bf16[1,128,1,8,128]{4,1,3,2,0:T(8,128)(2,1)S(1)} %get-tuple-element.15), channel_id=1, source_target_pairs={{0,32},{32,64},{64,96},{96,128},{128,160},{160,192},{192,224},{224... | collective-permute-start | bytes 786440 | tf_op jit(solution)/shard_map/ppermute | solution.py:14
  47.5 8.7 %collective-permute-start.1 = (bf16[1,128,1,8,128]{4,1,3,2,0:T(8,128)(2,1)S(1)}, bf16[1,128,1,8,128]{4,1,3,2,0:T(8,128)(2,1)S(1)}, u32[]{:S(2)}, u32[]{:S(2)}) collective-permute-start(bf16[1,128,1,8,128]{4,1,3,2,0:T(8,128)(2,1)S(1)} %get-tuple-element.16), channel_id=1, source_target_pairs={{32,0},{64,32},{96,64},{128,96},{160,128},{192,160},{224,192},{0,2... | collective-permute-start | bytes 786440 | tf_op jit(solution)/shard_map/ppermute | solution.py:16
  55.9 5.1 %copy-start.2 = (bf16[3,3,3,32,128]{4,3,2,1,0:T(8,128)(2,1)S(1)}, bf16[3,3,3,32,128]{4,3,2,1,0:T(8,128)(2,1)}, u32[]{:S(2)}) copy-start(bf16[3,3,3,32,128]{4,3,2,1,0:T(8,128)(2,1)} %param.6) | copy-start | bytes 663556
  56.3 18.3 %collective-permute-start.3 = (bf16[1,128,10,1,128]{4,1,3,2,0:T(8,128)(2,1)S(1)}, bf16[1,128,10,1,128]{4,1,3,2,0:T(8,128)(2,1)S(1)}, u32[]{:S(2)}, u32[]{:S(2)}) collective-permute-start(bf16[1,128,10,1,128]{4,1,3,2,0:T(8,128)(2,1)S(1)} %get-tuple-element.11), channel_id=1, source_target_pairs={{4,0},{8,4},{12,8},{16,12},{20,16},{24,20},{28,24},{0,28},{5,1},{9... | collective-permute-start | bytes 983048 | tf_op jit(solution)/shard_map/ppermute | solution.py:16
  61.0 11.9 %collective-permute-start.2 = (bf16[1,128,10,1,128]{4,1,3,2,0:T(8,128)(2,1)S(1)}, bf16[1,128,10,1,128]{4,1,3,2,0:T(8,128)(2,1)S(1)}, u32[]{:S(2)}, u32[]{:S(2)}) collective-permute-start(bf16[1,128,10,1,128]{4,1,3,2,0:T(8,128)(2,1)S(1)} %get-tuple-element.12), channel_id=1, source_target_pairs={{0,4},{4,8},{8,12},{12,16},{16,20},{20,24},{24,28},{28,0},{1,5},{5... | collective-permute-start | bytes 983048 | tf_op jit(solution)/shard_map/ppermute | solution.py:14
  82.8 0.7 copy-start.4
  83.5 36.8 %copy-start.3 = (bf16[3,3,3,32,128]{4,3,2,1,0:T(8,128)(2,1)S(1)}, bf16[3,3,3,32,128]{4,3,2,1,0:T(8,128)(2,1)}, u32[]{:S(2)}) copy-start(bf16[3,3,3,32,128]{4,3,2,1,0:T(8,128)(2,1)} %param.8) | copy-start | bytes 663556
  116.9 9.8 %copy-start.1 = (bf16[1,128,8,8,128]{4,1,3,2,0:T(8,128)(2,1)S(1)}, bf16[1,128,8,8,128]{4,1,3,2,0:T(8,128)(2,1)}, u32[]{:S(2)}) copy-start(bf16[1,128,8,8,128]{4,1,3,2,0:T(8,128)(2,1)} %all-gather.5.cloned.1.call-done) | copy-start | bytes 6291460
  116.9 9.7 %collective-permute-start.4 = (bf16[1,128,1,8,128]{4,1,3,2,0:T(8,128)(2,1)S(1)}, bf16[1,128,1,8,128]{4,1,3,2,0:T(8,128)(2,1)S(1)}, u32[]{:S(2)}, u32[]{:S(2)}) collective-permute-start(bf16[1,128,1,8,128]{4,1,3,2,0:T(8,128)(2,1)S(1)} %get-tuple-element.13), channel_id=1, source_target_pairs={{0,32},{32,64},{64,96},{96,128},{128,160},{160,192},{192,224},{224... | collective-permute-start | bytes 786440 | tf_op jit(solution)/shard_map/ppermute | solution.py:14
  118.3 8.7 %collective-permute-start.5 = (bf16[1,128,1,8,128]{4,1,3,2,0:T(8,128)(2,1)S(1)}, bf16[1,128,1,8,128]{4,1,3,2,0:T(8,128)(2,1)S(1)}, u32[]{:S(2)}, u32[]{:S(2)}) collective-permute-start(bf16[1,128,1,8,128]{4,1,3,2,0:T(8,128)(2,1)S(1)} %get-tuple-element.14), channel_id=1, source_target_pairs={{32,0},{64,32},{96,64},{128,96},{160,128},{192,160},{224,192},{0,2... | collective-permute-start | bytes 786440 | tf_op jit(solution)/shard_map/ppermute | solution.py:16
  127.0 19.9 %collective-permute-start.7 = (bf16[1,128,10,1,128]{4,1,3,2,0:T(8,128)(2,1)S(1)}, bf16[1,128,10,1,128]{4,1,3,2,0:T(8,128)(2,1)S(1)}, u32[]{:S(2)}, u32[]{:S(2)}) collective-permute-start(bf16[1,128,10,1,128]{4,1,3,2,0:T(8,128)(2,1)S(1)} %get-tuple-element.9), channel_id=1, source_target_pairs={{4,0},{8,4},{12,8},{16,12},{20,16},{24,20},{28,24},{0,28},{5,1},{9... | collective-permute-start | bytes 983048 | tf_op jit(solution)/shard_map/ppermute | solution.py:16
  131.7 11.9 %collective-permute-start.6 = (bf16[1,128,10,1,128]{4,1,3,2,0:T(8,128)(2,1)S(1)}, bf16[1,128,10,1,128]{4,1,3,2,0:T(8,128)(2,1)S(1)}, u32[]{:S(2)}, u32[]{:S(2)}) collective-permute-start(bf16[1,128,10,1,128]{4,1,3,2,0:T(8,128)(2,1)S(1)} %get-tuple-element.10), channel_id=1, source_target_pairs={{0,4},{4,8},{8,12},{12,16},{16,20},{20,24},{24,28},{28,0},{1,5},{5... | collective-permute-start | bytes 983048 | tf_op jit(solution)/shard_map/ppermute | solution.py:14
  156.6 0.7 copy-start.5
Sparse Core Ops, SparseCore 0:
  9.2 35.8 all-gather.2
  86.4 29.3 all-gather.4
where the time goes:
time: 167 us; the launch traced here: 166 us
  waiting for transfers between devices  92.6 us (55%)
  matrix products  30.8 us (18%)
  starting transfers between devices  15.9 us (10%)
  between operations  13.7 us (8%)
  local copies, waits for them, and re-layouts  9.39 us (6%)
  other arithmetic  3.36 us (2%)
    all_gather x2, waiting for transfers between devices, conv_layer(): gathered = lax.all_gather(volume, 'col', axis=1, tiled=True)  65.8 us
    dot_general x18, matrix products, depth_terms(): jnp.einsum('bixyz,doi->bdoxyz', slab, weight[step_x, step_y], preferred_e...  30.8 us
    ppermute x4, waiting for transfers between devices, with_halo(): lax.ppermute(tail, axis, [(i, (i + 1) % count) for i in range(count)])  26.7 us
    ppermute x4, starting transfers between devices, with_halo(): lax.ppermute(head, axis, [((i + 1) % count, i) for i in range(count)])  13.2 us
    convert_element_type x2, other arithmetic, finish(): jax.nn.relu(total + layer_bias[None, :, None, None, None])  3.36 us
  transfers between devices with their start and end apart: 10, of which 6 were waited for; matrix products, arithmetic and copies ran while one was open for 9% of the time, Pallas kernels for 0%

commit v1 on v0

v1 whole, which is shorter than its diff:
```python
import jax
import jax.numpy as jnp
from jax import lax
from jax.experimental import pallas as pl
from jax.experimental.pallas import tpu as pltpu
from jax.sharding import PartitionSpec as P

BF16 = jnp.bfloat16
F32 = jnp.float32
MESH = pl.DeviceIdType.MESH
MATES = ((1, 0), (0, 1), (1, 1))
AROUND = ((-1, 0), (1, 0), (0, -1), (0, 1), (-1, -1), (-1, 1), (1, -1), (1, 1))
TAPS = tuple((dx, dy) for dx in range(3) for dy in range(3))


def mo(value, unit):
    return pl.multiple_of(value, unit)


def kernel(
    vol, w1, w2, b1, b2, out,
    part, cells, hidden, weights, bias_part, bias, result, final,
    local_sem, mate_s, mate_r, ext_s, ext_r, w_s, w_r, b_s, b_r, h_s, h_r, o_s, o_r,
):
    gx, gy, col = lax.axis_index("gx"), lax.axis_index("gy"), lax.axis_index("col")
    a, k = col // 2, col % 2
    xs, ys = (a + gx) % 2, (k + gy) % 2
    big_x, big_y = 2 * gx + xs, 2 * gy + ys
    mine = mo(32 * col, 32)

    def at(to_x, to_y):
        to_x, to_y = (to_x + 16) % 16, (to_y + 16) % 16
        tx, ty = to_x // 2, to_y // 2
        return tx, ty, 2 * ((to_x % 2 + tx) % 2) + (to_y % 2 + ty) % 2

    around = [at(big_x + dx, big_y + dy) for dx, dy in AROUND]
    mates = [(gx, gy, 2 * ((a + fx) % 2) + (k + fy) % 2) for fx, fy in MATES]
    across = [(gx, (gy + 4) % 8, 2 * (1 - a) + (k + d) % 2) for d in range(2)]
    w_to = [mates[1]] + across

    barrier = pltpu.get_barrier_semaphore()
    for device in around + across:
        pl.semaphore_signal(barrier, inc=1, device_id=device, device_id_type=MESH)

    def remote(src, dst, s, r, device):
        return pltpu.make_async_remote_copy(
            src_ref=src, dst_ref=dst, send_sem=s, recv_sem=r, device_id=device, device_id_type=MESH
        )

    own_w = [
        pltpu.make_async_copy(w, weights.at[l, :, pl.ds(mine, 32), :], local_sem.at[l])
        for l, w in enumerate((w1, w2))
    ]
    for c in own_w:
        c.start()

    for x in range(8):
        rows = jnp.swapaxes(vol[:, x], 0, 1)
        for y in range(8):
            part[x, :, y * 128 : (y + 1) * 128] = rows[y]
    eye = lax.broadcasted_iota(jnp.int32, (32, 32), 0) == lax.broadcasted_iota(jnp.int32, (32, 32), 1)
    for l, b in enumerate((b1, b2)):
        column = jnp.sum(jnp.where(eye, b[...], 0.0), axis=1, keepdims=True)
        bias_part[:, l * 64 : (l + 1) * 64] = jnp.broadcast_to(column, (32, 64))

    pl.semaphore_wait(barrier, len(around) + len(across))

    def block(xq, yq):
        return part.at[pl.ds(3 * xq, 5), :, pl.ds(mo(384 * yq, 128), 640)]

    def place(xq, yq):
        return cells.at[pl.ds(1 - xq, 5), pl.ds(mine, 32), pl.ds(mo(128 * (1 - yq), 128), 640)]

    mate_copies = []
    for i, (fx, fy) in enumerate(MATES):
        xq, yq = (xs + fx) % 2, (ys + fy) % 2
        c = remote(block(xq, yq), place(xq, yq), mate_s.at[i], mate_r.at[i], mates[i])
        c.start()
        mate_copies.append(c)
    own_cells = pltpu.make_async_copy(block(xs, ys), place(xs, ys), local_sem.at[2])
    own_cells.start()
    own_bias = pltpu.make_async_copy(bias_part, bias.at[pl.ds(mine, 32), :], local_sem.at[3])
    own_bias.start()
    w_copies = [[], []]
    b_copies = []
    for i in range(3):
        c = remote(bias_part, bias.at[pl.ds(mine, 32), :], b_s.at[i], b_r.at[i], mates[i])
        c.start()
        b_copies.append(c)
    for l, w in enumerate((w1, w2)):
        for i in range(3):
            c = remote(w, weights.at[l, :, pl.ds(mine, 32), :], w_s.at[l, i], w_r.at[l, i], w_to[i])
            c.start()
            w_copies[l].append(c)

    own_cells.wait()
    for c in mate_copies:
        c.wait_recv()

    row, col_at = 1 + 3 * xs, mo(128 * (1 + 3 * ys), 128)
    row_to, col_to = 5 * (1 - xs), mo(640 * (1 - ys), 128)
    rows5, lanes5 = pl.ds(1 - xs, 5), pl.ds(mo(128 * (1 - ys), 128), 640)
    ext = [
        remote(
            cells.at[pl.ds(row, 1), :, lanes5], cells.at[pl.ds(row_to, 1), :, lanes5],
            ext_s.at[0], ext_r.at[0], at(big_x + 2 * xs - 1, big_y),
        ),
        remote(
            cells.at[rows5, :, pl.ds(col_at, 128)], cells.at[rows5, :, pl.ds(col_to, 128)],
            ext_s.at[1], ext_r.at[1], at(big_x, big_y + 2 * ys - 1),
        ),
        remote(
            cells.at[pl.ds(row, 1), :, pl.ds(col_at, 128)], cells.at[pl.ds(row_to, 1), :, pl.ds(col_to, 128)],
            ext_s.at[2], ext_r.at[2], at(big_x + 2 * xs - 1, big_y + 2 * ys - 1),
        ),
    ]
    for c in ext:
        c.start()

    own_bias.wait()
    for c in b_copies:
        c.wait_recv()
    own_w[0].wait()
    for c in w_copies[0]:
        c.wait_recv()
    for c in ext:
        c.wait_recv()

    def conv(source, l, x):
        stacked = jnp.concatenate(
            [
                jnp.concatenate([weights[l, (dx * 3 + dy) * 3 + dz] for dx, dy in TAPS], axis=1)
                for dz in range(3)
            ],
            axis=0,
        )
        shift = bias[:, l * 64 : l * 64 + 1]
        pieces = []
        for y in (0, 2):
            right = jnp.concatenate(
                [source[x + dx, :, (y + dy) * 128 : (y + dy + 2) * 128] for dx, dy in TAPS], axis=0
            )
            terms = jnp.dot(stacked, right, preferred_element_type=F32)
            for j in range(2):
                t = terms[:, j * 128 : (j + 1) * 128]
                total = pltpu.roll(t[0:128], 1, axis=1) + t[128:256] + pltpu.roll(t[256:384], 127, axis=1)
                pieces.append(jnp.maximum(total + shift, 0.0).astype(BF16))
        return pieces

    def first(x):
        for y, piece in enumerate(conv(cells, 0, x)):
            hidden[x + 1, :, (y + 1) * 128 : (y + 2) * 128] = piece

    def halo(i):
        dx, dy = AROUND[i]
        spans = {-1: (1, 5), 1: (4, 0)}
        fx, tx = spans.get(dx, (1, 1))
        fy, ty = spans.get(dy, (1, 1))
        nx, ny = (1 if dx else 4), (128 if dy else 512)
        return remote(
            hidden.at[pl.ds(fx, nx), :, pl.ds(fy * 128, ny)],
            hidden.at[pl.ds(tx, nx), :, pl.ds(ty * 128, ny)],
            h_s.at[i], h_r.at[i], around[i],
        )

    halos = [halo(i) for i in range(8)]

    @pl.loop(0, 2)
    def _(i):
        first(3 * i)

    for i in (0, 1, 4, 5, 6, 7):
        halos[i].start()

    @pl.loop(1, 3)
    def _(i):
        first(i)

    for i in (2, 3):
        halos[i].start()

    own_w[1].wait()
    for c in w_copies[1]:
        c.wait_recv()
    for c in halos:
        c.wait_recv()

    def spread(x, i):
        other = 2 * ((a + MATES[i][0]) % 2) + (k + MATES[i][1]) % 2
        return remote(
            result.at[pl.ds(x, 1), pl.ds(mo(32 * other, 32), 32), :],
            final.at[pl.ds(4 * xs + x, 1), :, pl.ds(mo(512 * ys, 512), 512)],
            o_s.at[i, x], o_r.at[i, x], mates[i],
        )

    def own_result():
        return pltpu.make_async_copy(
            result.at[:, pl.ds(mine, 32), :],
            final.at[pl.ds(4 * xs, 4), :, pl.ds(mo(512 * ys, 512), 512)],
            local_sem.at[4],
        )

    @pl.loop(0, 4)
    def _(x):
        for y, piece in enumerate(conv(hidden, 1, x)):
            result[x, :, y * 128 : (y + 1) * 128] = piece
        for i in range(3):
            spread(x, i).start()

    own_result().start()
    own_result().wait()
    for x in range(4):
        for i in range(3):
            spread(x, i).wait_recv()

    for x in range(8):
        rows = jnp.stack([final[x, :, y * 128 : (y + 1) * 128] for y in range(8)], axis=0)
        out[:, x] = jnp.swapaxes(rows, 0, 1)

    for c in mate_copies + b_copies + w_copies[0] + w_copies[1] + ext + halos:
        c.wait_send()
    for x in range(4):
        for i in range(3):
            spread(x, i).wait_send()


def local(volume, weight_one, bias_one, weight_two, bias_two):
    vmem = pl.BlockSpec(memory_space=pltpu.VMEM)
    hbm = pl.BlockSpec(memory_space=pl.ANY)
    dma = pltpu.SemaphoreType.DMA
    out = pl.pallas_call(
        kernel,
        out_shape=jax.ShapeDtypeStruct((32, 8, 8, 128), BF16),
        in_specs=[vmem, hbm, hbm, vmem, vmem],
        out_specs=vmem,
        scratch_shapes=[
            pltpu.VMEM((8, 32, 1024), BF16),
            pltpu.VMEM((6, 128, 768), BF16),
            pltpu.VMEM((6, 128, 768), BF16),
            pltpu.VMEM((2, 27, 128, 128), BF16),
            pltpu.VMEM((32, 128), F32),
            pltpu.VMEM((128, 128), F32),
            pltpu.VMEM((4, 128, 512), BF16),
            pltpu.VMEM((8, 32, 1024), BF16),
            dma((5,)),
            dma((3,)), dma((3,)),
            dma((3,)), dma((3,)),
            dma((2, 3)), dma((2, 3)),
            dma((3,)), dma((3,)),
            dma((8,)), dma((8,)),
            dma((3, 4)), dma((3, 4)),
        ],
        compiler_params=pltpu.CompilerParams(
            collective_id=0, has_side_effects=True, vmem_limit_bytes=48 * 2**20
        ),
        cost_estimate=pl.CostEstimate(flops=3_700_000_000, bytes_accessed=3_000_000, transcendentals=0),
    )(
        volume.reshape(32, 8, 8, 128),
        weight_one.reshape(27, 32, 128),
        weight_two.reshape(27, 32, 128),
        bias_one.reshape(1, 32),
        bias_two.reshape(1, 32),
    )
    return out.reshape(1, 32, 8, 8, 128)


def solution(mesh):
    in_specs = (
        P(None, "col", "gx", "gy", None),
        P(None, None, None, "col", None),
        P("col"),
        P(None, None, None, "col", None),
        P("col"),
    )
    out_specs = P(None, "col", "gx", "gy", None)
    return jax.shard_map(local, mesh=mesh, in_specs=in_specs, out_specs=out_specs, check_vma=False)
```

time: 167 us -> 49.7 us (0.30)
  waiting for transfers between devices: 92.6 us -> 0 us
  Pallas kernels: 0 us -> 45.1 us
  matrix products: 30.8 us -> 0 us
  starting transfers between devices: 15.9 us -> 0 us
  between operations: 13.7 us -> 0.01 us
  local copies, waits for them, and re-layouts: 9.39 us -> 4.38 us
  other arithmetic: 3.36 us -> 0 us
    all_gather x2 -> x0, waiting for transfers between devices: 65.8 us -> none  [conv_layer(): gathered = lax.all_gather(volume, 'col', axis=1, tiled=True)]
    pallas_call x0 -> x1, Pallas kernels: none -> 45.1 us  [local(): pl.pallas_call(kernel, out_shape=jax.ShapeDtypeStruct((32, 8, 8, 128), BF...]
    dot_general x18 -> x0, matrix products: 30.8 us -> none  [depth_terms(): jnp.einsum('bixyz,doi->bdoxyz', slab, weight[step_x, step_y], preferred_e...]
    ppermute x8 -> x0, waiting for transfers between devices: 26.7 us -> none  [the longest x4 26.7 us: with_halo(): lax.ppermute(tail, axis, [(i, (i + 1) % count) for i in range(count)])]
    ppermute x8 -> x0, starting transfers between devices: 15.9 us -> none  [the longest x4 13.2 us: with_halo(): lax.ppermute(head, axis, [((i + 1) % count, i) for i in range(count)])]
    slice x8 -> x0, local copies, waits for them, and re-layouts: 3.59 us -> none  [the longest x2 2.13 us: with_halo(): lax.slice_in_dim(cells, cells.shape[dim] - width, cells.shape[dim], axis=...]
    convert_element_type x2 -> x0, other arithmetic: 3.36 us -> none  [finish(): jax.nn.relu(total + layer_bias[None, :, None, None, None])]
    squeeze x2 -> x0, local copies, waits for them, and re-layouts: 1.94 us -> none  [local_conv(): terms[:, 2]]
  transfers between devices with their start and end apart: 10 -> 0, of which waited for: 6 -> 0; matrix products, arithmetic and copies ran while one was open for 9% -> 0% of each run, Pallas kernels for 0% -> 0%
where the time goes in v1:
time: 49.7 us; the launch traced here: 49.5 us
  Pallas kernels  45.1 us (91%)
  local copies, waits for them, and re-layouts  4.38 us (9%)
    pallas_call x1, Pallas kernels, local(): pl.pallas_call(kernel, out_shape=jax.ShapeDtypeStruct((32, 8, 8, 128), BF...  45.1 us
    unnamed x11, local copies, waits for them, and re-layouts  4.38 us

profile of v1, /device:TPU:1, one launch (start us, length us, event | category | flops | bytes accessed | tf_op | source)
XLA Modules:
  0.0 49.5 jit_solution(14215408426512264293)
XLA Ops:
  0.0 0.0 copy-start.3
  0.0 0.0 copy-start.4
  0.0 0.7 %copy-done.3 = f32[32]{0:T(128)S(1)} copy-done((f32[32]{0:T(128)S(1)}, f32[32]{0:T(128)}, u32[]{:S(2)}) %copy-start.3) | copy-done | bytes 152
  0.7 0.0 copy-done.4
  0.7 0.0 copy-start
  0.7 1.0 %copy-done = bf16[1,32,8,8,128]{4,3,2,1,0:T(8,128)(2,1)S(1)} copy-done((bf16[1,32,8,8,128]{4,3,2,1,0:T(8,128)(2,1)S(1)}, bf16[1,32,8,8,128]{4,3,2,1,0:T(8,128)(2,1)}, u32[]{:S(2)}) %copy-start) | copy-done | bytes 524312
  1.7 0.0 copy-start.1
  1.7 0.9 %copy-done.1 = bf16[3,3,3,32,128]{4,3,2,1,0:T(8,128)(2,1)S(1)} copy-done((bf16[3,3,3,32,128]{4,3,2,1,0:T(8,128)(2,1)S(1)}, bf16[3,3,3,32,128]{4,3,2,1,0:T(8,128)(2,1)}, u32[]{:S(2)}) %copy-start.1) | copy-done | bytes 221208
  2.7 0.0 copy-start.2
  2.7 0.9 %copy-done.2 = bf16[3,3,3,32,128]{4,3,2,1,0:T(8,128)(2,1)S(1)} copy-done((bf16[3,3,3,32,128]{4,3,2,1,0:T(8,128)(2,1)S(1)}, bf16[3,3,3,32,128]{4,3,2,1,0:T(8,128)(2,1)}, u32[]{:S(2)}) %copy-start.2) | copy-done | bytes 221208
  3.6 45.1 %shard_map.55 = bf16[32,8,8,128]{3,2,1,0:T(8,128)(2,1)S(1)} custom-call(bf16[32,8,8,128]{3,2,1,0:T(8,128)(2,1)S(1)} %bitcast.7, bf16[27,32,128]{2,1,0:T(8,128)(2,1)S(1)} %bitcast.8, bf16[27,32,128]{2,1,0:T(8,128)(2,1)S(1)} %bitcast.9, f32[1,32]{1,0:T(1,128)S(1)} %bitcast.10, f32[1,32]{1,0:T(1,128)S(1)} %bitcast.11), custom_call_target="tpu_custom_call" | custom-call | flops 3700000000 | bytes 3000000 | tf_op jit(solution)/shard_map/pallas_call | solution.py:231
  48.7 0.8 %copy.7 = bf16[1,32,8,8,128]{4,3,2,1,0:T(8,128)(2,1)} copy(bf16[1,32,8,8,128]{4,3,2,1,0:T(8,128)(2,1)S(1)} %bitcast.6) | data formatting | bytes 1048576
Async XLA Ops:
  0.0 0.7 %copy-start.3 = (f32[32]{0:T(128)S(1)}, f32[32]{0:T(128)}, u32[]{:S(2)}) copy-start(f32[32]{0:T(128)} %param.7) | copy-start | bytes 388
  0.0 0.7 %copy-start.4 = (f32[32]{0:T(128)S(1)}, f32[32]{0:T(128)}, u32[]{:S(2)}) copy-start(f32[32]{0:T(128)} %param.9) | copy-start | bytes 388
  0.7 1.0 %copy-start = (bf16[1,32,8,8,128]{4,3,2,1,0:T(8,128)(2,1)S(1)}, bf16[1,32,8,8,128]{4,3,2,1,0:T(8,128)(2,1)}, u32[]{:S(2)}) copy-start(bf16[1,32,8,8,128]{4,3,2,1,0:T(8,128)(2,1)} %param.5) | copy-start | bytes 1572868
  1.7 0.9 %copy-start.1 = (bf16[3,3,3,32,128]{4,3,2,1,0:T(8,128)(2,1)S(1)}, bf16[3,3,3,32,128]{4,3,2,1,0:T(8,128)(2,1)}, u32[]{:S(2)}) copy-start(bf16[3,3,3,32,128]{4,3,2,1,0:T(8,128)(2,1)} %param.6) | copy-start | bytes 663556
  2.7 0.9 %copy-start.2 = (bf16[3,3,3,32,128]{4,3,2,1,0:T(8,128)(2,1)S(1)}, bf16[3,3,3,32,128]{4,3,2,1,0:T(8,128)(2,1)}, u32[]{:S(2)}) copy-start(bf16[3,3,3,32,128]{4,3,2,1,0:T(8,128)(2,1)} %param.8) | copy-start | bytes 663556

commit v2 on v1

v2 whole, which is shorter than its diff:
```python
import jax
import jax.numpy as jnp
from jax import lax
from jax.experimental import pallas as pl
from jax.experimental.pallas import tpu as pltpu
from jax.sharding import PartitionSpec as P

BF16 = jnp.bfloat16
F32 = jnp.float32
MESH = pl.DeviceIdType.MESH
MATES = ((1, 0), (1, 1), (0, 1))
AROUND = ((-1, 0), (1, 0), (0, -1), (0, 1), (-1, -1), (-1, 1), (1, -1), (1, 1))
TAPS = tuple((dx, dy) for dx in range(3) for dy in range(3))


def mo(value, unit):
    return pl.multiple_of(value, unit)


def kernel(
    vol_in, w1, w2, b1_in, b2_in, out,
    vol, b1, b2, part, cells, hidden, weights, bias_part, bias, result, final,
    in_sem, own_sem, mate_s, mate_r, ext_s, ext_r, w_s, w_r, b_s, b_r, h_s, h_r, o_s, o_r,
):
    gx, gy, col = lax.axis_index("gx"), lax.axis_index("gy"), lax.axis_index("col")
    a, k = col // 2, col % 2
    xs, ys = (a + gx) % 2, (k + gy) % 2
    big_x, big_y = 2 * gx + xs, 2 * gy + ys
    mine = mo(32 * col, 32)

    def at(to_x, to_y):
        to_x, to_y = (to_x + 16) % 16, (to_y + 16) % 16
        tx, ty = to_x // 2, to_y // 2
        return tx, ty, 2 * ((to_x % 2 + tx) % 2) + (to_y % 2 + ty) % 2

    around = [at(big_x + dx, big_y + dy) for dx, dy in AROUND]
    mates = [(gx, gy, 2 * ((a + fx) % 2) + (k + fy) % 2) for fx, fy in MATES]
    sibling = mates[2]
    across = (gx, (gy + 4) % 8, 2 * (1 - a) + k)

    barrier = pltpu.get_barrier_semaphore()
    for device in around + [across]:
        pl.semaphore_signal(barrier, inc=1, device_id=device, device_id_type=MESH)

    def remote(src, dst, s, r, device):
        return pltpu.make_async_remote_copy(
            src_ref=src, dst_ref=dst, send_sem=s, recv_sem=r, device_id=device, device_id_type=MESH
        )

    fetch = [
        pltpu.make_async_copy(src, dst, in_sem.at[i])
        for i, (src, dst) in enumerate(((vol_in, vol), (b1_in, b1), (b2_in, b2)))
    ]
    own_w = [
        pltpu.make_async_copy(w, weights.at[l, :, pl.ds(mine, 32), :], in_sem.at[3 + l])
        for l, w in enumerate((w1, w2))
    ]
    for c in fetch + own_w:
        c.start()
    for c in fetch:
        c.wait()

    for x in range(8):
        rows = jnp.swapaxes(vol[:, x], 0, 1)
        for y in range(8):
            part[x, :, y * 128 : (y + 1) * 128] = rows[y]
    eye = lax.broadcasted_iota(jnp.int32, (32, 32), 0) == lax.broadcasted_iota(jnp.int32, (32, 32), 1)
    for l, b in enumerate((b1, b2)):
        column = jnp.sum(jnp.where(eye, b[...], 0.0), axis=1, keepdims=True)
        bias_part[:, l * 64 : (l + 1) * 64] = jnp.broadcast_to(column, (32, 64))

    pl.semaphore_wait(barrier, len(around) + 1)

    def piece(x0, nx, y0, ny, to_x, to_y):
        return (
            part.at[pl.ds(x0, nx), :, pl.ds(mo(128 * y0, 128), 128 * ny)],
            cells.at[pl.ds(to_x, nx), pl.ds(mine, 32), pl.ds(128 * to_y, 128 * ny)],
        )

    early, late = [], []
    for i in range(2):
        xq, yq = (xs + MATES[i][0]) % 2, (ys + MATES[i][1]) % 2
        pieces = (
            piece(7 * xq, 1, 4 * yq, 4, 1 + 3 * xq, 1),
            piece(1 + 2 * xq, 4, 4 * yq, 1, 2 - 2 * xq, 1),
            piece(1 + 2 * xq, 4, 4 * yq + 3, 1, 2 - 2 * xq, 4),
            piece(1 + 2 * xq, 4, 4 * yq + 1, 2, 2 - 2 * xq, 2),
        )
        copies = [remote(s, d, mate_s.at[i, j], mate_r.at[i, j], mates[i]) for j, (s, d) in enumerate(pieces)]
        early.extend(copies[:3])
        late.append(copies[3])
    src, dst = piece(3 * xs, 5, 4 * ((ys + 1) % 2), 4, 1 - xs, 1)
    near = remote(src, dst, mate_s.at[2, 0], mate_r.at[2, 0], sibling)
    src, dst = piece(3 * xs, 5, 4 * ys, 4, 1 - xs, 1)
    own_cells = pltpu.make_async_copy(src, dst, own_sem.at[0])
    own_bias = pltpu.make_async_copy(bias_part, bias.at[pl.ds(mine, 32), :], own_sem.at[1])
    w_far, w_near, w_on = [], [], []
    theirs = mo(64 * (1 - a) + 32 * k, 32)
    for l, w in enumerate((w1, w2)):
        slot, other = weights.at[l, :, pl.ds(mine, 32), :], weights.at[l, :, pl.ds(theirs, 32), :]
        w_far.append(remote(w, slot, w_s.at[l, 0], w_r.at[l, 0], across))
        w_near.append(remote(w, slot, w_s.at[l, 1], w_r.at[l, 1], sibling))
        w_on.append(remote(other, other, w_s.at[l, 2], w_r.at[l, 2], sibling))
    b_copies = [
        remote(bias_part, bias.at[pl.ds(mine, 32), :], b_s.at[i], b_r.at[i], mates[i]) for i in range(3)
    ]

    own_cells.start()
    near.start()
    for c in early:
        c.start()
    w_far[0].start()
    w_near[0].start()
    own_bias.start()
    for c in late:
        c.start()
    for c in b_copies:
        c.start()

    row, row_to = 1 + 3 * xs, 5 * (1 - xs)
    rows5 = pl.ds(1 - xs, 5)
    x_out = big_x + 2 * xs - 1

    def edges(j):
        half = pl.ds(mo(64 * (a if j == 0 else 1 - a), 64), 64)
        spots = (
            (pl.ds(row, 1), pl.ds(row_to, 1), 128, 128, 512, at(x_out, big_y)),
            (rows5, rows5, 512, 0, 128, at(big_x, big_y + 1)),
            (rows5, rows5, 128, 640, 128, at(big_x, big_y - 1)),
            (pl.ds(row, 1), pl.ds(row_to, 1), 512, 0, 128, at(x_out, big_y + 1)),
            (pl.ds(row, 1), pl.ds(row_to, 1), 128, 640, 128, at(x_out, big_y - 1)),
        )
        return [
            remote(
                cells.at[rf, half, pl.ds(lf, n)], cells.at[rt, half, pl.ds(lt, n)],
                ext_s.at[j, i], ext_r.at[j, i], device,
            )
            for i, (rf, rt, lf, lt, n, device) in enumerate(spots)
        ]

    ext = [edges(0), edges(1)]
    own_cells.wait()
    near.wait_recv()
    for c in ext[0]:
        c.start()
    for c in early:
        c.wait_recv()
    for c in ext[1]:
        c.start()
    w_far[0].wait_recv()
    w_on[0].start()
    w_far[1].start()
    w_near[1].start()
    own_bias.wait()
    for c in own_w:
        c.wait()
    for c in b_copies + late + [w_near[0]] + ext[0] + ext[1] + [w_on[0]]:
        c.wait_recv()

    def conv(source, l, x):
        stacked = jnp.concatenate(
            [
                jnp.concatenate([weights[l, (dx * 3 + dy) * 3 + dz] for dx, dy in TAPS], axis=1)
                for dz in range(3)
            ],
            axis=0,
        )
        shift = bias[:, l * 64 : l * 64 + 1]
        pieces = []
        for y in (0, 2):
            right = jnp.concatenate(
                [source[x + dx, :, (y + dy) * 128 : (y + dy + 2) * 128] for dx, dy in TAPS], axis=0
            )
            terms = jnp.dot(stacked, right, preferred_element_type=F32)
            for j in range(2):
                t = terms[:, j * 128 : (j + 1) * 128]
                total = pltpu.roll(t[0:128], 1, axis=1) + t[128:256] + pltpu.roll(t[256:384], 127, axis=1)
                pieces.append(jnp.maximum(total + shift, 0.0).astype(BF16))
        return pieces

    def first(x):
        for y, value in enumerate(conv(cells, 0, x)):
            hidden[x + 1, :, (y + 1) * 128 : (y + 2) * 128] = value

    def halo(i, from_x, nx, from_y, ny, to_x, to_y, device):
        return remote(
            hidden.at[pl.ds(from_x, nx), :, pl.ds(from_y * 128, ny * 128)],
            hidden.at[pl.ds(to_x, nx), :, pl.ds(to_y * 128, ny * 128)],
            h_s.at[i], h_r.at[i], device,
        )

    x_low, x_high, y_low, y_high, ll, lh, hl, hh = around
    outer = [
        halo(0, 1, 1, 1, 4, 5, 1, x_low),
        halo(1, 4, 1, 1, 4, 0, 1, x_high),
        halo(2, 1, 1, 1, 1, 5, 5, ll),
        halo(3, 1, 1, 4, 1, 5, 0, lh),
        halo(4, 4, 1, 1, 1, 0, 5, hl),
        halo(5, 4, 1, 4, 1, 0, 0, hh),
    ]
    sides = [
        [
            halo(6 + 2 * j, x, n, 1, 1, x, 5, y_low),
            halo(7 + 2 * j, x, n, 4, 1, x, 0, y_high),
        ]
        for j, (x, n) in enumerate(((1, 1), (4, 1), (2, 2)))
    ]

    @pl.loop(0, 2)
    def _(i):
        first(3 * i)

    for c in outer[:2] + sides[0] + sides[1] + outer[2:]:
        c.start()

    @pl.loop(1, 3)
    def _(i):
        first(i)

    for c in sides[2]:
        c.start()
    w_far[1].wait_recv()
    w_on[1].start()
    for pair in sides:
        for c in pair:
            c.wait_recv()
    w_near[1].wait_recv()
    w_on[1].wait_recv()

    def spread(x, i):
        other = 2 * ((a + MATES[i][0]) % 2) + (k + MATES[i][1]) % 2
        return remote(
            result.at[pl.ds(x, 1), pl.ds(mo(32 * other, 32), 32), :],
            final.at[pl.ds(4 * xs + x, 1), :, pl.ds(mo(512 * ys, 512), 512)],
            o_s.at[i, x], o_r.at[i, x], mates[i],
        )

    def own_result(x):
        return pltpu.make_async_copy(
            result.at[pl.ds(x, 1), pl.ds(mine, 32), :],
            final.at[pl.ds(4 * xs + x, 1), :, pl.ds(mo(512 * ys, 512), 512)],
            own_sem.at[2 + x],
        )

    def second(x):
        for y, value in enumerate(conv(hidden, 1, x)):
            result[x, :, y * 128 : (y + 1) * 128] = value
        for i in range(3):
            spread(x, i).start()
        own_result(x).start()

    @pl.loop(1, 3)
    def _(x):
        second(x)

    for c in outer:
        c.wait_recv()

    @pl.loop(0, 2)
    def _(x):
        second(3 * x)

    for x in (1, 2, 0, 3):
        own_result(x).wait()
        for i in range(3):
            spread(x, i).wait_recv()
        for at_x in (x, x + 4):
            rows = jnp.stack([final[at_x, :, y * 128 : (y + 1) * 128] for y in range(8)], axis=0)
            out[:, at_x] = jnp.swapaxes(rows, 0, 1)

    for c in early + late + [near] + b_copies + w_far + w_near + w_on + ext[0] + ext[1] + outer:
        c.wait_send()
    for pair in sides:
        for c in pair:
            c.wait_send()
    for x in range(4):
        for i in range(3):
            spread(x, i).wait_send()


def local(volume, weight_one, bias_one, weight_two, bias_two):
    vmem = pl.BlockSpec(memory_space=pltpu.VMEM)
    hbm = pl.BlockSpec(memory_space=pl.ANY)
    dma = pltpu.SemaphoreType.DMA
    out = pl.pallas_call(
        kernel,
        out_shape=jax.ShapeDtypeStruct((32, 8, 8, 128), BF16),
        in_specs=[hbm] * 5,
        out_specs=vmem,
        scratch_shapes=[
            pltpu.VMEM((32, 8, 8, 128), BF16),
            pltpu.VMEM((1, 32), F32),
            pltpu.VMEM((1, 32), F32),
            pltpu.VMEM((8, 32, 1024), BF16),
            pltpu.VMEM((6, 128, 768), BF16),
            pltpu.VMEM((6, 128, 768), BF16),
            pltpu.VMEM((2, 27, 128, 128), BF16),
            pltpu.VMEM((32, 128), F32),
            pltpu.VMEM((128, 128), F32),
            pltpu.VMEM((4, 128, 512), BF16),
            pltpu.VMEM((8, 32, 1024), BF16),
            dma((5,)), dma((6,)),
            dma((3, 4)), dma((3, 4)),
            dma((2, 5)), dma((2, 5)),
            dma((2, 3)), dma((2, 3)),
            dma((3,)), dma((3,)),
            dma((12,)), dma((12,)),
            dma((3, 4)), dma((3, 4)),
        ],
        compiler_params=pltpu.CompilerParams(
            collective_id=0, has_side_effects=True, vmem_limit_bytes=60 * 2**20
        ),
        cost_estimate=pl.CostEstimate(flops=3_700_000_000, bytes_accessed=3_000_000, transcendentals=0),
    )(
        volume.reshape(32, 8, 8, 128),
        weight_one.reshape(27, 32, 128),
        weight_two.reshape(27, 32, 128),
        bias_one.reshape(1, 32),
        bias_two.reshape(1, 32),
    )
    return out.reshape(1, 32, 8, 8, 128)


def solution(mesh):
    in_specs = (
        P(None, "col", "gx", "gy", None),
        P(None, None, None, "col", None),
        P("col"),
        P(None, None, None, "col", None),
        P("col"),
    )
    out_specs = P(None, "col", "gx", "gy", None)
    return jax.shard_map(local, mesh=mesh, in_specs=in_specs, out_specs=out_specs, check_vma=False)
```

time: 49.7 us -> 41.1 us (0.83)
  Pallas kernels: 45.1 us -> 39.1 us
  local copies, waits for them, and re-layouts: 4.38 us -> 1.87 us
    pallas_call x1, Pallas kernels: 45.1 us -> 39.1 us  [local(): pl.pallas_call(kernel, out_shape=jax.ShapeDtypeStruct((32, 8, 8, 128), BF...]
    unnamed x11 -> x1, local copies, waits for them, and re-layouts: 4.38 us -> 1.87 us
where the time goes in v2:
time: 41.1 us; the launch traced here: 41 us
  Pallas kernels  39.1 us (95%)
  local copies, waits for them, and re-layouts  1.87 us (5%)
    pallas_call x1, Pallas kernels, local(): pl.pallas_call(kernel, out_shape=jax.ShapeDtypeStruct((32, 8, 8, 128), BF...  39.1 us
    unnamed x1, local copies, waits for them, and re-layouts  1.87 us

profile of v2, /device:TPU:1, one launch (start us, length us, event | category | flops | bytes accessed | tf_op | source)
XLA Modules:
  0.0 41.0 jit_solution(14000295159056101700)
XLA Ops:
  0.0 39.1 %shard_map.55 = bf16[32,8,8,128]{3,2,1,0:T(8,128)(2,1)} custom-call(bf16[32,8,8,128]{3,2,1,0:T(8,128)(2,1)} %bitcast.7, bf16[27,32,128]{2,1,0:T(8,128)(2,1)} %bitcast.8, bf16[27,32,128]{2,1,0:T(8,128)(2,1)} %bitcast.9, f32[1,32]{1,0:T(1,128)} %bitcast.10, f32[1,32]{1,0:T(1,128)} %bitcast.11), custom_call_target="tpu_custom_call" | custom-call | flops 3700000000 | bytes 3000000 | tf_op jit(solution)/shard_map/pallas_call | solution.py:285
  39.1 1.9 %copy.7 = bf16[1,32,8,8,128]{4,3,2,1,0:T(8,128)(2,1)} copy(bf16[1,32,8,8,128]{4,3,2,1,0:T(8,128)(2,1)} %bitcast.6) | data formatting | bytes 1048576

commit v3 on v2

v3 whole, which is shorter than its diff:
```python
import jax
import jax.numpy as jnp
from jax import lax
from jax.experimental import pallas as pl
from jax.experimental.pallas import tpu as pltpu
from jax.sharding import PartitionSpec as P

BF16 = jnp.bfloat16
F32 = jnp.float32
MESH = pl.DeviceIdType.MESH
MATES = ((1, 0), (1, 1), (0, 1))


def mo(value, unit):
    return pl.multiple_of(value, unit)


def kernel(
    vol_in, w1, w2, b1_in, b2_in, out,
    vol, b1, b2, part, cells, hidden, weights, bias_part, bias, result, final,
    in_sem, own_sem, mate_s, mate_r, ext_s, ext_r, w_s, w_r, b_s, b_r, h_s, h_r, o_s, o_r,
):
    gx, gy, col = lax.axis_index("gx"), lax.axis_index("gy"), lax.axis_index("col")
    a, k = col // 2, col % 2
    xs, ys = (a + gx + gy // 4) % 2, (k + gy) % 2
    big_x, big_y = 2 * gx + xs, 2 * gy + ys
    mine = mo(32 * col, 32)

    def at(to_x, to_y):
        to_x, to_y = (to_x + 16) % 16, (to_y + 16) % 16
        tx, ty = to_x // 2, to_y // 2
        return tx, ty, 2 * ((to_x % 2 + tx + ty // 4) % 2) + (to_y % 2 + ty) % 2

    mates = [(gx, gy, 2 * ((a + fx) % 2) + (k + fy) % 2) for fx, fy in MATES]
    sibling = mates[2]
    across = (gx, (gy + 4) % 8, 2 * (1 - a) + k)
    x_next = at(big_x + 2 * xs - 1, big_y)
    y_next = at(big_x, big_y + 2 * ys - 1)
    y_pair = at(big_x, big_y + 1), at(big_x, big_y - 1)
    next_pair = at(big_x + 2 * xs - 1, big_y + 1), at(big_x + 2 * xs - 1, big_y - 1)
    mate_pair = at(big_x + 1 - 2 * xs, big_y + 1), at(big_x + 1 - 2 * xs, big_y - 1)
    far_corner = at(big_x + 1 - 2 * xs, big_y + 2 * ys - 1)

    barrier = pltpu.get_barrier_semaphore()
    partners = mates + [across, x_next, y_next, far_corner, next_pair[0], next_pair[1]]
    for device in partners:
        pl.semaphore_signal(barrier, inc=1, device_id=device, device_id_type=MESH)

    def remote(src, dst, s, r, device):
        return pltpu.make_async_remote_copy(
            src_ref=src, dst_ref=dst, send_sem=s, recv_sem=r, device_id=device, device_id_type=MESH
        )

    fetch = [
        pltpu.make_async_copy(src, dst, in_sem.at[i])
        for i, (src, dst) in enumerate(((vol_in, vol), (b1_in, b1), (b2_in, b2)))
    ]
    own_w = [
        pltpu.make_async_copy(w, weights.at[l, :, pl.ds(mine, 32), :], in_sem.at[3 + l])
        for l, w in enumerate((w1, w2))
    ]
    for c in fetch + own_w:
        c.start()
    for c in fetch:
        c.wait()

    for x in range(8):
        rows = jnp.swapaxes(vol[:, x], 0, 1)
        for y in range(8):
            part[x, :, y * 128 : (y + 1) * 128] = rows[y]
    eye = lax.broadcasted_iota(jnp.int32, (32, 32), 0) == lax.broadcasted_iota(jnp.int32, (32, 32), 1)
    for l, b in enumerate((b1, b2)):
        column = jnp.sum(jnp.where(eye, b[...], 0.0), axis=1, keepdims=True)
        bias_part[:, l * 64 : (l + 1) * 64] = jnp.broadcast_to(column, (32, 64))

    pl.semaphore_wait(barrier, len(partners))

    def piece(x0, nx, y0, ny, to_x, to_y):
        return (
            part.at[pl.ds(x0, nx), :, pl.ds(mo(128 * y0, 128), 128 * ny)],
            cells.at[pl.ds(to_x, nx), pl.ds(mine, 32), pl.ds(128 * to_y, 128 * ny)],
        )

    early, late = [], []
    for i in range(2):
        xq, yq = (xs + MATES[i][0]) % 2, (ys + MATES[i][1]) % 2
        pieces = (
            piece(7 * xq, 1, 4 * yq, 4, 1 + 3 * xq, 1),
            piece(1 + 2 * xq, 4, 4 * yq, 1, 2 - 2 * xq, 1),
            piece(1 + 2 * xq, 4, 4 * yq + 3, 1, 2 - 2 * xq, 4),
            piece(1 + 2 * xq, 4, 4 * yq + 1, 2, 2 - 2 * xq, 2),
        )
        copies = [remote(s, d, mate_s.at[i, j], mate_r.at[i, j], mates[i]) for j, (s, d) in enumerate(pieces)]
        early.extend(copies[:3])
        late.append(copies[3])
    src, dst = piece(3 * xs, 5, 4 * ((ys + 1) % 2), 4, 1 - xs, 1)
    near = remote(src, dst, mate_s.at[2, 0], mate_r.at[2, 0], sibling)
    src, dst = piece(3 * xs, 5, 4 * ys, 4, 1 - xs, 1)
    own_cells = pltpu.make_async_copy(src, dst, own_sem.at[0])
    own_bias = pltpu.make_async_copy(bias_part, bias.at[pl.ds(mine, 32), :], own_sem.at[1])
    theirs = mo(64 * (1 - a) + 32 * k, 32)

    def send_w(l, w, first_tap, n_taps, i, device):
        slot = weights.at[l, pl.ds(first_tap, n_taps), pl.ds(mine, 32), :]
        return remote(w.at[pl.ds(first_tap, n_taps)], slot, w_s.at[i], w_r.at[i], device)

    def pass_w(l, i):
        slot = weights.at[l, :, pl.ds(theirs, 32), :]
        return remote(slot, slot, w_s.at[i], w_r.at[i], sibling)

    w1_far, w1_near, w1_on = send_w(0, w1, 0, 27, 0, across), send_w(0, w1, 0, 27, 1, sibling), pass_w(0, 2)
    w2_far = [send_w(1, w2, 0, 14, 3, mates[0]), send_w(1, w2, 14, 13, 4, across)]
    w2_near, w2_on = send_w(1, w2, 0, 27, 5, sibling), pass_w(1, 6)
    b_copies = [
        remote(bias_part, bias.at[pl.ds(mine, 32), :], b_s.at[i], b_r.at[i], mates[i]) for i in range(3)
    ]

    own_cells.start()
    near.start()
    for c in early:
        c.start()
    w1_far.start()
    w1_near.start()
    own_bias.start()
    for c in late:
        c.start()
    for c in b_copies:
        c.start()

    end, end_to = 1 + 3 * xs, 5 * (1 - xs)
    rows5 = pl.ds(1 - xs, 5)

    def edges(j):
        half = pl.ds(mo(64 * (a if j == 0 else 1 - a), 64), 64)
        spots = (
            (pl.ds(end, 1), pl.ds(end_to, 1), 128, 128, 512, x_next),
            (rows5, rows5, 512, 0, 128, y_pair[0]),
            (rows5, rows5, 128, 640, 128, y_pair[1]),
            (pl.ds(end, 1), pl.ds(end_to, 1), 512, 0, 128, next_pair[0]),
            (pl.ds(end, 1), pl.ds(end_to, 1), 128, 640, 128, next_pair[1]),
        )
        return [
            remote(
                cells.at[rf, half, pl.ds(lf, n)], cells.at[rt, half, pl.ds(lt, n)],
                ext_s.at[j, i], ext_r.at[j, i], device,
            )
            for i, (rf, rt, lf, lt, n, device) in enumerate(spots)
        ]

    ext = [edges(0), edges(1)]
    own_cells.wait()
    near.wait_recv()
    for c in ext[0]:
        c.start()
    for c in early:
        c.wait_recv()
    for c in ext[1]:
        c.start()
    w1_far.wait_recv()
    w1_on.start()
    w2_far[1].start()
    for c in late:
        c.wait_recv()
    w2_far[0].start()
    w2_near.start()
    own_bias.wait()
    for c in own_w:
        c.wait()
    for c in b_copies + [w1_near] + ext[0][1:3] + ext[1][1:3] + [w1_on]:
        c.wait_recv()

    def conv(source, l, x, dxs):
        stacked = jnp.concatenate(
            [
                jnp.concatenate([weights[l, dx * 9 + (dy * 3 + dz)] for dx in dxs for dy in range(3)], axis=1)
                for dz in range(3)
            ],
            axis=0,
        )
        totals = []
        for y in (0, 2):
            right = jnp.concatenate(
                [source[x + dx, :, (y + dy) * 128 : (y + dy + 2) * 128] for dx in dxs for dy in range(3)], axis=0
            )
            terms = jnp.dot(stacked, right, preferred_element_type=F32)
            for j in range(2):
                t = terms[:, j * 128 : (j + 1) * 128]
                totals.append(pltpu.roll(t[0:128], 1, axis=1) + t[128:256] + pltpu.roll(t[256:384], 127, axis=1))
        return totals

    def finish(total, l):
        return jnp.maximum(total + bias[:, l * 64 : l * 64 + 1], 0.0).astype(BF16)

    def line(t, side=None):
        q = xs if side is None else side
        return t + q * (3 - 2 * t)

    def first(t):
        x = line(t)
        for y, total in enumerate(conv(cells, 0, x, (0, 1, 2))):
            hidden[x + 1, :, (y + 1) * 128 : (y + 2) * 128] = finish(total, 0)

    def halo(i, x, to_x, device):
        return remote(
            hidden.at[pl.ds(x, 1), :, pl.ds(128, 512)], hidden.at[pl.ds(to_x, 1), :, pl.ds(128, 512)],
            h_s.at[i], h_r.at[i], device,
        )

    def columns(i, x, to_x, devices):
        return [
            remote(
                hidden.at[pl.ds(x, 1), :, pl.ds(lf, 128)], hidden.at[pl.ds(to_x, 1), :, pl.ds(lt, 128)],
                h_s.at[i + j], h_r.at[i + j], device,
            )
            for j, (lf, lt, device) in enumerate(((512, 0, devices[0]), (128, 640, devices[1])))
        ]

    to_mate = [halo(0, 1 + line(3), 5 * xs, mates[0])] + columns(1, 1 + line(3), 5 * xs, mate_pair)
    to_next = [halo(3, 1 + line(0), 5 * (1 - xs), x_next)] + columns(4, 1 + line(0), 5 * (1 - xs), next_pair)
    side = [columns(6 + 2 * t, 1 + line(t), 1 + line(t), y_pair) for t in range(4)]

    for j in (0, 1):
        for i in (0, 3, 4):
            ext[j][i].wait_recv()
    first(0)
    for c in to_next + side[0]:
        c.start()
    first(3)
    for c in to_mate + side[3]:
        c.start()
    first(1)
    for c in side[1]:
        c.start()
    for c in w2_far:
        c.wait_recv()
    w2_on.start()
    first(2)
    for c in side[2]:
        c.start()

    def spread(t, i):
        other = 2 * ((a + MATES[i][0]) % 2) + (k + MATES[i][1]) % 2
        return remote(
            result.at[pl.ds(line(t), 1), pl.ds(mo(32 * other, 32), 32), :],
            final.at[pl.ds(4 * xs + line(t), 1), :, pl.ds(mo(512 * ys, 512), 512)],
            o_s.at[i, t], o_r.at[i, t], mates[i],
        )

    def own_result(t):
        return pltpu.make_async_copy(
            result.at[pl.ds(line(t), 1), pl.ds(mine, 32), :],
            final.at[pl.ds(4 * xs + line(t), 1), :, pl.ds(mo(512 * ys, 512), 512)],
            own_sem.at[2 + t],
        )

    spreads = [[spread(t, i) for i in range(3)] for t in range(4)]
    own_results = [own_result(t) for t in range(4)]

    def second(t, totals):
        for y, total in enumerate(totals):
            result[line(t), :, y * 128 : (y + 1) * 128] = finish(total, 1)
        for c in spreads[t]:
            c.start()
        own_results[t].start()

    w2_near.wait_recv()
    w2_on.wait_recv()
    for t in (0, 3, 1, 2):
        for c in side[t]:
            c.wait_recv()
    second(1, conv(hidden, 1, line(1), (0, 1, 2)))
    second(2, conv(hidden, 1, line(2), (0, 1, 2)))
    for c in to_next:
        c.wait_recv()
    second(0, conv(hidden, 1, line(0), (0, 1, 2)))
    for c in to_mate:
        c.wait_recv()
    second(3, conv(hidden, 1, line(3), (0, 1, 2)))

    for t in (1, 2, 0, 3):
        own_results[t].wait()
        for c in spreads[t]:
            c.wait_recv()
        for x in (4 * xs + line(t), 4 * (1 - xs) + line(t, 1 - xs)):
            rows = jnp.stack([final[x, :, y * 128 : (y + 1) * 128] for y in range(8)], axis=0)
            out[:, pl.ds(x, 1)] = jnp.swapaxes(rows, 0, 1)[:, None]

    sent = early + late + [near] + b_copies + [w1_far, w1_near, w1_on, w2_near, w2_on] + w2_far
    sent += ext[0] + ext[1] + to_mate + to_next
    for t in range(4):
        sent += side[t] + spreads[t]
    for c in sent:
        c.wait_send()


def local(volume, weight_one, bias_one, weight_two, bias_two):
    vmem = pl.BlockSpec(memory_space=pltpu.VMEM)
    hbm = pl.BlockSpec(memory_space=pl.ANY)
    dma = pltpu.SemaphoreType.DMA
    out = pl.pallas_call(
        kernel,
        out_shape=pltpu.VMEM((32, 8, 8, 128), BF16),
        in_specs=[hbm] * 5,
        out_specs=vmem,
        scratch_shapes=[
            pltpu.VMEM((32, 8, 8, 128), BF16),
            pltpu.VMEM((1, 32), F32),
            pltpu.VMEM((1, 32), F32),
            pltpu.VMEM((8, 32, 1024), BF16),
            pltpu.VMEM((6, 128, 768), BF16),
            pltpu.VMEM((6, 128, 768), BF16),
            pltpu.VMEM((2, 27, 128, 128), BF16),
            pltpu.VMEM((32, 128), F32),
            pltpu.VMEM((128, 128), F32),
            pltpu.VMEM((4, 128, 512), BF16),
            pltpu.VMEM((8, 32, 1024), BF16),
            dma((5,)), dma((6,)),
            dma((3, 4)), dma((3, 4)),
            dma((2, 5)), dma((2, 5)),
            dma((7,)), dma((7,)),
            dma((3,)), dma((3,)),
            dma((14,)), dma((14,)),
            dma((3, 4)), dma((3, 4)),
        ],
        compiler_params=pltpu.CompilerParams(
            collective_id=0, has_side_effects=True, vmem_limit_bytes=60 * 2**20
        ),
        cost_estimate=pl.CostEstimate(flops=3_700_000_000, bytes_accessed=3_000_000, transcendentals=0),
    )(
        volume.reshape(32, 8, 8, 128),
        weight_one.reshape(27, 32, 128),
        weight_two.reshape(27, 32, 128),
        bias_one.reshape(1, 32),
        bias_two.reshape(1, 32),
    )
    return out.reshape(1, 32, 8, 8, 128)


def solution(mesh):
    in_specs = (
        P(None, "col", "gx", "gy", None),
        P(None, None, None, "col", None),
        P("col"),
        P(None, None, None, "col", None),
        P("col"),
    )
    out_specs = P(None, "col", "gx", "gy", None)
    return jax.shard_map(local, mesh=mesh, in_specs=in_specs, out_specs=out_specs, check_vma=False)
```

time: 41.1 us -> 36.3 us (0.88); the launches traced: 41 us -> 35.8 us
  Pallas kernels: 39.1 us -> 35 us
  local copies, waits for them, and re-layouts: 1.87 us -> 0.8 us
    pallas_call x1, Pallas kernels: 39.1 us -> 35 us  [local(): pl.pallas_call(kernel, out_shape=pltpu.VMEM((32, 8, 8, 128), BF16), in_sp...]
    unnamed x1, local copies, waits for them, and re-layouts: 1.87 us -> 0.8 us
where the time goes in v3:
time: 36.3 us; the launch traced here: 35.8 us
  Pallas kernels  35 us (96%)
  local copies, waits for them, and re-layouts  0.8 us (2%)
    pallas_call x1, Pallas kernels, local(): pl.pallas_call(kernel, out_shape=pltpu.VMEM((32, 8, 8, 128), BF16), in_sp...  35 us
    unnamed x1, local copies, waits for them, and re-layouts  0.8 us

profile of v3, /device:TPU:1, one launch (start us, length us, event | category | flops | bytes accessed | tf_op | source)
XLA Modules:
  0.0 35.8 jit_solution(12232961354974565910)
XLA Ops:
  0.0 35.0 %shard_map.55 = bf16[32,8,8,128]{3,2,1,0:T(8,128)(2,1)S(1)} custom-call(bf16[32,8,8,128]{3,2,1,0:T(8,128)(2,1)} %bitcast.7, bf16[27,32,128]{2,1,0:T(8,128)(2,1)} %bitcast.8, bf16[27,32,128]{2,1,0:T(8,128)(2,1)} %bitcast.9, f32[1,32]{1,0:T(1,128)} %bitcast.10, f32[1,32]{1,0:T(1,128)} %bitcast.11), custom_call_target="tpu_custom_call" | custom-call | flops 3700000000 | bytes 3000000 | tf_op jit(solution)/shard_map/pallas_call | solution.py:300
  35.0 0.8 %copy.7 = bf16[1,32,8,8,128]{4,3,2,1,0:T(8,128)(2,1)} copy(bf16[1,32,8,8,128]{4,3,2,1,0:T(8,128)(2,1)S(1)} %bitcast.6) | data formatting | bytes 1048576

commit v4 on v3

--- a/solution.py
+++ b/solution.py
@@ -39,10 +39,9 @@
     y_pair = at(big_x, big_y + 1), at(big_x, big_y - 1)
     next_pair = at(big_x + 2 * xs - 1, big_y + 1), at(big_x + 2 * xs - 1, big_y - 1)
     mate_pair = at(big_x + 1 - 2 * xs, big_y + 1), at(big_x + 1 - 2 * xs, big_y - 1)
-    far_corner = at(big_x + 1 - 2 * xs, big_y + 2 * ys - 1)
 
     barrier = pltpu.get_barrier_semaphore()
-    partners = mates + [across, x_next, y_next, far_corner, next_pair[0], next_pair[1]]
+    partners = mates + [across, x_next, y_next]
     for device in partners:
         pl.semaphore_signal(barrier, inc=1, device_id=device, device_id_type=MESH)
 
@@ -136,8 +135,6 @@
             (pl.ds(end, 1), pl.ds(end_to, 1), 128, 128, 512, x_next),
             (rows5, rows5, 512, 0, 128, y_pair[0]),
             (rows5, rows5, 128, 640, 128, y_pair[1]),
-            (pl.ds(end, 1), pl.ds(end_to, 1), 512, 0, 128, next_pair[0]),
-            (pl.ds(end, 1), pl.ds(end_to, 1), 128, 640, 128, next_pair[1]),
         )
         return [
             remote(
@@ -148,6 +145,13 @@
         ]
 
     ext = [edges(0), edges(1)]
+    corners = [
+        remote(
+            cells.at[pl.ds(end, 1), :, pl.ds(lf, 128)], cells.at[pl.ds(end_to, 1), :, pl.ds(lt, 128)],
+            ext_s.at[2, i], ext_r.at[2, i], device,
+        )
+        for i, (lf, lt, device) in enumerate(((512, 0, next_pair[0]), (128, 640, next_pair[1])))
+    ]
     own_cells.wait()
     near.wait_recv()
     for c in ext[0]:
@@ -155,6 +159,10 @@
     for c in early:
         c.wait_recv()
     for c in ext[1]:
+        c.start()
+    for c in ext[0][1:]:
+        c.wait_recv()
+    for c in corners:
         c.start()
     w1_far.wait_recv()
     w1_on.start()
@@ -166,27 +174,8 @@
     own_bias.wait()
     for c in own_w:
         c.wait()
-    for c in b_copies + [w1_near] + ext[0][1:3] + ext[1][1:3] + [w1_on]:
-        c.wait_recv()
-
-    def conv(source, l, x, dxs):
-        stacked = jnp.concatenate(
-            [
-                jnp.concatenate([weights[l, dx * 9 + (dy * 3 + dz)] for dx in dxs for dy in range(3)], axis=1)
-                for dz in range(3)
-            ],
-            axis=0,
-        )
-        totals = []
-        for y in (0, 2):
-            right = jnp.concatenate(
-                [source[x + dx, :, (y + dy) * 128 : (y + dy + 2) * 128] for dx in dxs for dy in range(3)], axis=0
-            )
-            terms = jnp.dot(stacked, right, preferred_element_type=F32)
-            for j in range(2):
-                t = terms[:, j * 128 : (j + 1) * 128]
-                totals.append(pltpu.roll(t[0:128], 1, axis=1) + t[128:256] + pltpu.roll(t[256:384], 127, axis=1))
-        return totals
+    for c in b_copies + [w1_near, w1_on]:
+        c.wait_recv()
 
     def finish(total, l):
         return jnp.maximum(total + bias[:, l * 64 : l * 64 + 1], 0.0).astype(BF16)
@@ -195,10 +184,33 @@
         q = xs if side is None else side
         return t + q * (3 - 2 * t)
 
-    def first(t):
-        x = line(t)
-        for y, total in enumerate(conv(cells, 0, x, (0, 1, 2))):
-            hidden[x + 1, :, (y + 1) * 128 : (y + 2) * 128] = finish(total, 0)
+    def apply(left, right):
+        terms = jnp.dot(left, right, preferred_element_type=F32)
+        totals = []
+        for j in range(2):
+            t = terms[:, j * 128 : (j + 1) * 128]
+            totals.append(pltpu.roll(t[0:128], 1, axis=1) + t[128:256] + pltpu.roll(t[256:384], 127, axis=1))
+        return totals
+
+    def stack(l, taps):
+        return jnp.concatenate(
+            [jnp.concatenate([weights[l, 3 * q + dz] for q in taps], axis=1) for dz in range(3)], axis=0
+        )
+
+    def gather(source, spots):
+        return jnp.concatenate(
+            [
+                jnp.concatenate(
+                    [source[line(t) + q // 3, :, (y + q % 3) * 128 : (y + q % 3 + 1) * 128] for t, y in spots], axis=1
+                )
+                for q in range(9)
+            ],
+            axis=0,
+        )
+
+    def first(*spots):
+        for (t, y), total in zip(spots, apply(stack(0, range(9)), gather(cells, spots))):
+            hidden[line(t) + 1, :, (y + 1) * 128 : (y + 2) * 128] = finish(total, 0)
 
     def halo(i, x, to_x, device):
         return remote(
@@ -206,10 +218,10 @@
             h_s.at[i], h_r.at[i], device,
         )
 
-    def columns(i, x, to_x, devices):
+    def columns(i, x, to_x, devices, n=1):
         return [
             remote(
-                hidden.at[pl.ds(x, 1), :, pl.ds(lf, 128)], hidden.at[pl.ds(to_x, 1), :, pl.ds(lt, 128)],
+                hidden.at[pl.ds(x, n), :, pl.ds(lf, 128)], hidden.at[pl.ds(to_x, n), :, pl.ds(lt, 128)],
                 h_s.at[i + j], h_r.at[i + j], device,
             )
             for j, (lf, lt, device) in enumerate(((512, 0, devices[0]), (128, 640, devices[1])))
@@ -217,77 +229,90 @@
 
     to_mate = [halo(0, 1 + line(3), 5 * xs, mates[0])] + columns(1, 1 + line(3), 5 * xs, mate_pair)
     to_next = [halo(3, 1 + line(0), 5 * (1 - xs), x_next)] + columns(4, 1 + line(0), 5 * (1 - xs), next_pair)
-    side = [columns(6 + 2 * t, 1 + line(t), 1 + line(t), y_pair) for t in range(4)]
-
-    for j in (0, 1):
-        for i in (0, 3, 4):
-            ext[j][i].wait_recv()
-    first(0)
+    side = {t: columns(6 + 2 * t, 1 + line(t), 1 + line(t), y_pair) for t in (0, 3)}
+    side[1] = columns(8, 2, 2, y_pair, 2)
+
+    first((3, 1), (3, 2))
+    first((1, 1), (1, 2))
+    first((2, 1), (2, 2))
+    for c in ext[1] + [ext[0][0]] + corners:
+        c.wait_recv()
+    first((0, 0), (0, 1))
+    first((0, 2), (0, 3))
     for c in to_next + side[0]:
         c.start()
-    first(3)
+    first((3, 0), (3, 3))
     for c in to_mate + side[3]:
         c.start()
-    first(1)
+    first((1, 0), (2, 0))
+    first((1, 3), (2, 3))
     for c in side[1]:
         c.start()
     for c in w2_far:
         c.wait_recv()
     w2_on.start()
-    first(2)
-    for c in side[2]:
-        c.start()
-
-    def spread(t, i):
+
+    def spread(x, n, i, slot):
         other = 2 * ((a + MATES[i][0]) % 2) + (k + MATES[i][1]) % 2
         return remote(
-            result.at[pl.ds(line(t), 1), pl.ds(mo(32 * other, 32), 32), :],
-            final.at[pl.ds(4 * xs + line(t), 1), :, pl.ds(mo(512 * ys, 512), 512)],
-            o_s.at[i, t], o_r.at[i, t], mates[i],
-        )
-
-    def own_result(t):
+            result.at[pl.ds(x, n), pl.ds(mo(32 * other, 32), 32), :],
+            final.at[pl.ds(4 * xs + x, n), :, pl.ds(mo(512 * ys, 512), 512)],
+            o_s.at[i, slot], o_r.at[i, slot], mates[i],
+        )
+
+    def own_result(x, n, slot):
         return pltpu.make_async_copy(
-            result.at[pl.ds(line(t), 1), pl.ds(mine, 32), :],
-            final.at[pl.ds(4 * xs + line(t), 1), :, pl.ds(mo(512 * ys, 512), 512)],
-            own_sem.at[2 + t],
-        )
-
-    spreads = [[spread(t, i) for i in range(3)] for t in range(4)]
-    own_results = [own_result(t) for t in range(4)]
-
-    def second(t, totals):
-        for y, total in enumerate(totals):
+            result.at[pl.ds(x, n), pl.ds(mine, 32), :],
+            final.at[pl.ds(4 * xs + x, n), :, pl.ds(mo(512 * ys, 512), 512)],
+            own_sem.at[2 + slot],
+        )
+
+    spans = {0: (line(0), 1), 1: (1, 2), 3: (line(3), 1)}
+    spreads = {t: [spread(x, n, i, t) for i in range(3)] for t, (x, n) in spans.items()}
+    own_results = {t: own_result(x, n, t) for t, (x, n) in spans.items()}
+
+    def second(*spots):
+        for (t, y), total in zip(spots, apply(stack(1, range(9)), gather(hidden, spots))):
             result[line(t), :, y * 128 : (y + 1) * 128] = finish(total, 1)
-        for c in spreads[t]:
-            c.start()
-        own_results[t].start()
+
+    def send_out(*lines):
+        for t in lines:
+            for c in spreads[t]:
+                c.start()
+            own_results[t].start()
 
     w2_near.wait_recv()
     w2_on.wait_recv()
-    for t in (0, 3, 1, 2):
+    second((1, 1), (1, 2))
+    second((2, 1), (2, 2))
+    for t in (0, 3, 1):
         for c in side[t]:
             c.wait_recv()
-    second(1, conv(hidden, 1, line(1), (0, 1, 2)))
-    second(2, conv(hidden, 1, line(2), (0, 1, 2)))
+    second((1, 0), (2, 0))
+    second((1, 3), (2, 3))
+    send_out(1)
     for c in to_next:
         c.wait_recv()
-    second(0, conv(hidden, 1, line(0), (0, 1, 2)))
+    second((0, 0), (0, 1))
+    second((0, 2), (0, 3))
+    send_out(0)
     for c in to_mate:
         c.wait_recv()
-    second(3, conv(hidden, 1, line(3), (0, 1, 2)))
-
-    for t in (1, 2, 0, 3):
+    second((3, 0), (3, 1))
+    second((3, 2), (3, 3))
+    send_out(3)
+
+    for t in (1, 0, 3):
         own_results[t].wait()
         for c in spreads[t]:
             c.wait_recv()
-        for x in (4 * xs + line(t), 4 * (1 - xs) + line(t, 1 - xs)):
+        for x in (1, 2, 5, 6) if t == 1 else (4 * xs + line(t), 4 * (1 - xs) + line(t, 1 - xs)):
             rows = jnp.stack([final[x, :, y * 128 : (y + 1) * 128] for y in range(8)], axis=0)
             out[:, pl.ds(x, 1)] = jnp.swapaxes(rows, 0, 1)[:, None]
 
     sent = early + late + [near] + b_copies + [w1_far, w1_near, w1_on, w2_near, w2_on] + w2_far
-    sent += ext[0] + ext[1] + to_mate + to_next
-    for t in range(4):
+    sent += ext[0] + ext[1] + corners + to_mate + to_next
+    for t in (0, 1, 3):
         sent += side[t] + spreads[t]
     for c in sent:
         c.wait_send()
@@ -316,7 +341,7 @@
             pltpu.VMEM((8, 32, 1024), BF16),
             dma((5,)), dma((6,)),
             dma((3, 4)), dma((3, 4)),
-            dma((2, 5)), dma((2, 5)),
+            dma((3, 3)), dma((3, 3)),
             dma((7,)), dma((7,)),
             dma((3,)), dma((3,)),
             dma((14,)), dma((14,)),

time: 36.3 us -> 35.6 us (0.981); the launches traced: 35.8 us -> 35.5 us
  no operation moved by 1% of the time
where the time goes in v4:
time: 35.6 us; the launch traced here: 35.5 us
  Pallas kernels  34.7 us (97%)
  local copies, waits for them, and re-layouts  0.8 us (2%)
    pallas_call x1, Pallas kernels, local(): pl.pallas_call(kernel, out_shape=pltpu.VMEM((32, 8, 8, 128), BF16), in_sp...  34.7 us
    unnamed x1, local copies, waits for them, and re-layouts  0.8 us

profile of v4, /device:TPU:1, one launch (start us, length us, event | category | flops | bytes accessed | tf_op | source)
XLA Modules:
  0.0 35.5 jit_solution(13626332741049308919)
XLA Ops:
  0.0 34.7 %shard_map.55 = bf16[32,8,8,128]{3,2,1,0:T(8,128)(2,1)S(1)} custom-call(bf16[32,8,8,128]{3,2,1,0:T(8,128)(2,1)} %bitcast.7, bf16[27,32,128]{2,1,0:T(8,128)(2,1)} %bitcast.8, bf16[27,32,128]{2,1,0:T(8,128)(2,1)} %bitcast.9, f32[1,32]{1,0:T(1,128)} %bitcast.10, f32[1,32]{1,0:T(1,128)} %bitcast.11), custom_call_target="tpu_custom_call" | custom-call | flops 3700000000 | bytes 3000000 | tf_op jit(solution)/shard_map/pallas_call | solution.py:325
  34.7 0.8 %copy.7 = bf16[1,32,8,8,128]{4,3,2,1,0:T(8,128)(2,1)} copy(bf16[1,32,8,8,128]{4,3,2,1,0:T(8,128)(2,1)S(1)} %bitcast.6) | data formatting | bytes 1048576

commit v5 on v4

--- a/solution.py
+++ b/solution.py
@@ -17,7 +17,7 @@
 
 def kernel(
     vol_in, w1, w2, b1_in, b2_in, out,
-    vol, b1, b2, part, cells, hidden, weights, bias_part, bias, result, final,
+    vol, b1, b2, part, cells, hidden, weights, bias_part, bias, sums, result, final,
     in_sem, own_sem, mate_s, mate_r, ext_s, ext_r, w_s, w_r, b_s, b_r, h_s, h_r, o_s, o_r,
 ):
     gx, gy, col = lax.axis_index("gx"), lax.axis_index("gy"), lax.axis_index("col")
@@ -64,9 +64,7 @@
         c.wait()
 
     for x in range(8):
-        rows = jnp.swapaxes(vol[:, x], 0, 1)
-        for y in range(8):
-            part[x, :, y * 128 : (y + 1) * 128] = rows[y]
+        part[x] = jnp.swapaxes(vol[:, x], 0, 1)
     eye = lax.broadcasted_iota(jnp.int32, (32, 32), 0) == lax.broadcasted_iota(jnp.int32, (32, 32), 1)
     for l, b in enumerate((b1, b2)):
         column = jnp.sum(jnp.where(eye, b[...], 0.0), axis=1, keepdims=True)
@@ -76,8 +74,8 @@
 
     def piece(x0, nx, y0, ny, to_x, to_y):
         return (
-            part.at[pl.ds(x0, nx), :, pl.ds(mo(128 * y0, 128), 128 * ny)],
-            cells.at[pl.ds(to_x, nx), pl.ds(mine, 32), pl.ds(128 * to_y, 128 * ny)],
+            part.at[pl.ds(x0, nx), pl.ds(y0, ny)],
+            cells.at[pl.ds(to_x, nx), pl.ds(to_y, ny), pl.ds(mine, 32)],
         )
 
     early, late = [], []
@@ -132,25 +130,25 @@
     def edges(j):
         half = pl.ds(mo(64 * (a if j == 0 else 1 - a), 64), 64)
         spots = (
-            (pl.ds(end, 1), pl.ds(end_to, 1), 128, 128, 512, x_next),
-            (rows5, rows5, 512, 0, 128, y_pair[0]),
-            (rows5, rows5, 128, 640, 128, y_pair[1]),
+            (pl.ds(end, 1), pl.ds(end_to, 1), 1, 1, 4, x_next),
+            (rows5, rows5, 4, 0, 1, y_pair[0]),
+            (rows5, rows5, 1, 5, 1, y_pair[1]),
         )
         return [
             remote(
-                cells.at[rf, half, pl.ds(lf, n)], cells.at[rt, half, pl.ds(lt, n)],
+                cells.at[rf, pl.ds(cf, n), half], cells.at[rt, pl.ds(ct, n), half],
                 ext_s.at[j, i], ext_r.at[j, i], device,
             )
-            for i, (rf, rt, lf, lt, n, device) in enumerate(spots)
+            for i, (rf, rt, cf, ct, n, device) in enumerate(spots)
         ]
 
     ext = [edges(0), edges(1)]
     corners = [
         remote(
-            cells.at[pl.ds(end, 1), :, pl.ds(lf, 128)], cells.at[pl.ds(end_to, 1), :, pl.ds(lt, 128)],
+            cells.at[pl.ds(end, 1), pl.ds(cf, 1)], cells.at[pl.ds(end_to, 1), pl.ds(ct, 1)],
             ext_s.at[2, i], ext_r.at[2, i], device,
         )
-        for i, (lf, lt, device) in enumerate(((512, 0, next_pair[0]), (128, 640, next_pair[1])))
+        for i, (cf, ct, device) in enumerate(((4, 0, next_pair[0]), (1, 5, next_pair[1])))
     ]
     own_cells.wait()
     near.wait_recv()
@@ -201,7 +199,7 @@
         return jnp.concatenate(
             [
                 jnp.concatenate(
-                    [source[line(t) + q // 3, :, (y + q % 3) * 128 : (y + q % 3 + 1) * 128] for t, y in spots], axis=1
+                    [source[line(t) + q // 3, y + q % 3] for t, y in spots], axis=1
                 )
                 for q in range(9)
             ],
@@ -210,21 +208,21 @@
 
     def first(*spots):
         for (t, y), total in zip(spots, apply(stack(0, range(9)), gather(cells, spots))):
-            hidden[line(t) + 1, :, (y + 1) * 128 : (y + 2) * 128] = finish(total, 0)
+            hidden[line(t) + 1, y + 1] = finish(total, 0)
 
     def halo(i, x, to_x, device):
         return remote(
-            hidden.at[pl.ds(x, 1), :, pl.ds(128, 512)], hidden.at[pl.ds(to_x, 1), :, pl.ds(128, 512)],
+            hidden.at[pl.ds(x, 1), pl.ds(1, 4)], hidden.at[pl.ds(to_x, 1), pl.ds(1, 4)],
             h_s.at[i], h_r.at[i], device,
         )
 
     def columns(i, x, to_x, devices, n=1):
         return [
             remote(
-                hidden.at[pl.ds(x, n), :, pl.ds(lf, 128)], hidden.at[pl.ds(to_x, n), :, pl.ds(lt, 128)],
+                hidden.at[pl.ds(x, n), pl.ds(cf, 1)], hidden.at[pl.ds(to_x, n), pl.ds(ct, 1)],
                 h_s.at[i + j], h_r.at[i + j], device,
             )
-            for j, (lf, lt, device) in enumerate(((512, 0, devices[0]), (128, 640, devices[1])))
+            for j, (cf, ct, device) in enumerate(((4, 0, devices[0]), (1, 5, devices[1])))
         ]
 
     to_mate = [halo(0, 1 + line(3), 5 * xs, mates[0])] + columns(1, 1 + line(3), 5 * xs, mate_pair)
@@ -255,15 +253,15 @@
     def spread(x, n, i, slot):
         other = 2 * ((a + MATES[i][0]) % 2) + (k + MATES[i][1]) % 2
         return remote(
-            result.at[pl.ds(x, n), pl.ds(mo(32 * other, 32), 32), :],
-            final.at[pl.ds(4 * xs + x, n), :, pl.ds(mo(512 * ys, 512), 512)],
+            result.at[pl.ds(x, n), :, pl.ds(mo(32 * other, 32), 32)],
+            final.at[pl.ds(4 * xs + x, n), pl.ds(4 * ys, 4)],
             o_s.at[i, slot], o_r.at[i, slot], mates[i],
         )
 
     def own_result(x, n, slot):
         return pltpu.make_async_copy(
-            result.at[pl.ds(x, n), pl.ds(mine, 32), :],
-            final.at[pl.ds(4 * xs + x, n), :, pl.ds(mo(512 * ys, 512), 512)],
+            result.at[pl.ds(x, n), :, pl.ds(mine, 32)],
+            final.at[pl.ds(4 * xs + x, n), pl.ds(4 * ys, 4)],
             own_sem.at[2 + slot],
         )
 
@@ -273,7 +271,26 @@
 
     def second(*spots):
         for (t, y), total in zip(spots, apply(stack(1, range(9)), gather(hidden, spots))):
-            result[line(t), :, y * 128 : (y + 1) * 128] = finish(total, 1)
+            result[line(t), y] = finish(total, 1)
+
+    def part_of(t, spots, dxs):
+        taps = [(dx, dy) for dx in dxs for dy in range(3)]
+        left = jnp.concatenate(
+            [jnp.concatenate([weights[1, dx * 9 + (3 * dy + dz)] for dx, dy in taps], axis=1) for dz in range(3)],
+            axis=0,
+        )
+        right = jnp.concatenate(
+            [jnp.concatenate([hidden[line(t) + dx, y + dy] for y in spots], axis=1) for dx, dy in taps], axis=0
+        )
+        return zip(spots, apply(left, right))
+
+    def begin(t, *spots):
+        for y, total in part_of(t, spots, (1 - xs, 2 - xs) if t == 0 else (xs, 1 + xs)):
+            sums[t // 3, y] = total
+
+    def close(t, *spots):
+        for y, total in part_of(t, spots, (2 * xs,) if t == 0 else (2 - 2 * xs,)):
+            result[line(t), y] = finish(total + sums[t // 3, y], 1)
 
     def send_out(*lines):
         for t in lines:
@@ -285,21 +302,25 @@
     w2_on.wait_recv()
     second((1, 1), (1, 2))
     second((2, 1), (2, 2))
+    begin(0, 1, 2)
+    begin(3, 1, 2)
     for t in (0, 3, 1):
         for c in side[t]:
             c.wait_recv()
     second((1, 0), (2, 0))
     second((1, 3), (2, 3))
     send_out(1)
+    begin(0, 0, 3)
+    begin(3, 0, 3)
     for c in to_next:
         c.wait_recv()
-    second((0, 0), (0, 1))
-    second((0, 2), (0, 3))
+    close(0, 1, 2)
+    close(0, 0, 3)
     send_out(0)
     for c in to_mate:
         c.wait_recv()
-    second((3, 0), (3, 1))
-    second((3, 2), (3, 3))
+    close(3, 1, 2)
+    close(3, 0, 3)
     send_out(3)
 
     for t in (1, 0, 3):
@@ -307,8 +328,7 @@
         for c in spreads[t]:
             c.wait_recv()
         for x in (1, 2, 5, 6) if t == 1 else (4 * xs + line(t), 4 * (1 - xs) + line(t, 1 - xs)):
-            rows = jnp.stack([final[x, :, y * 128 : (y + 1) * 128] for y in range(8)], axis=0)
-            out[:, pl.ds(x, 1)] = jnp.swapaxes(rows, 0, 1)[:, None]
+            out[:, pl.ds(x, 1)] = jnp.swapaxes(final[x], 0, 1)[:, None]
 
     sent = early + late + [near] + b_copies + [w1_far, w1_near, w1_on, w2_near, w2_on] + w2_far
     sent += ext[0] + ext[1] + corners + to_mate + to_next
@@ -331,14 +351,15 @@
             pltpu.VMEM((32, 8, 8, 128), BF16),
             pltpu.VMEM((1, 32), F32),
             pltpu.VMEM((1, 32), F32),
-            pltpu.VMEM((8, 32, 1024), BF16),
-            pltpu.VMEM((6, 128, 768), BF16),
-            pltpu.VMEM((6, 128, 768), BF16),
+            pltpu.VMEM((8, 8, 32, 128), BF16),
+            pltpu.VMEM((6, 6, 128, 128), BF16),
+            pltpu.VMEM((6, 6, 128, 128), BF16),
             pltpu.VMEM((2, 27, 128, 128), BF16),
             pltpu.VMEM((32, 128), F32),
             pltpu.VMEM((128, 128), F32),
-            pltpu.VMEM((4, 128, 512), BF16),
-            pltpu.VMEM((8, 32, 1024), BF16),
+            pltpu.VMEM((2, 4, 128, 128), F32),
+            pltpu.VMEM((4, 4, 128, 128), BF16),
+            pltpu.VMEM((8, 8, 32, 128), BF16),
             dma((5,)), dma((6,)),
             dma((3, 4)), dma((3, 4)),
             dma((3, 3)), dma((3, 3)),

time: 35.6 us -> 35.6 us (level)
  no operation moved by 1% of the time
where the time goes in v5:
time: 35.6 us; the launch traced here: 35.5 us
  Pallas kernels  34.7 us (97%)
  local copies, waits for them, and re-layouts  0.8 us (2%)
    pallas_call x1, Pallas kernels, local(): pl.pallas_call(kernel, out_shape=pltpu.VMEM((32, 8, 8, 128), BF16), in_sp...  34.7 us
    unnamed x1, local copies, waits for them, and re-layouts  0.8 us

profile of v5, /device:TPU:1, one launch (start us, length us, event | category | flops | bytes accessed | tf_op | source)
XLA Modules:
  0.0 35.5 jit_solution(16967235086207709304)
XLA Ops:
  0.0 34.7 %shard_map.55 = bf16[32,8,8,128]{3,2,1,0:T(8,128)(2,1)S(1)} custom-call(bf16[32,8,8,128]{3,2,1,0:T(8,128)(2,1)} %bitcast.7, bf16[27,32,128]{2,1,0:T(8,128)(2,1)} %bitcast.8, bf16[27,32,128]{2,1,0:T(8,128)(2,1)} %bitcast.9, f32[1,32]{1,0:T(1,128)} %bitcast.10, f32[1,32]{1,0:T(1,128)} %bitcast.11), custom_call_target="tpu_custom_call" | custom-call | flops 3700000000 | bytes 3000000 | tf_op jit(solution)/shard_map/pallas_call | solution.py:345
  34.7 0.8 %copy.7 = bf16[1,32,8,8,128]{4,3,2,1,0:T(8,128)(2,1)} copy(bf16[1,32,8,8,128]{4,3,2,1,0:T(8,128)(2,1)S(1)} %bitcast.6) | data formatting | bytes 1048576
